TPU v7x, 256 devices: a whole 4x4x8 slice. The times are simulated.
256 devices in a mesh: mem: 8 (over y, core), ctx: 32 (over z, x).
Axes of the slice: x: 4, y: 4, z: 8, core: 2. Of those that a mesh axis runs over, the one named last changes fastest.
Arguments:
- queries: bfloat16 [32, 1024, 32, 128], P('ctx', 'mem'), may hold values from -6 to 6
- keys: bfloat16 [32, 1024, 32, 128], P('ctx', 'mem'), may hold values from -6 to 6
- values: bfloat16 [32, 1024, 32, 128], P('ctx', 'mem'), may hold values from -6 to 6
- log_decay: bfloat16 [32, 1024, 32], P('ctx', 'mem'), may hold values from -1 to 0, as said below
- routes: int32 [32, 1024, 2], P('ctx', 'mem'), may hold values from 0 to 7, all different within a row; in each aligned block of 128 rows (0 to 127, 128 to 255, ..., all dimensions but the last counted through in order) at most 40 rows name the same one
- route_weight: float32 [32, 1024, 2], P('ctx', 'mem'), may hold values from 0.2 to 1
- gain: float32 [4096], replicated, may hold values from 0.25 to 1.75
Outputs:
- layer_out: bfloat16 [32, 1024, 32, 128], P('ctx', 'mem')
Inputs may be any that keep to these rules, and one draw needn't show every extreme that they name: `routes`: A token's two memories differ. Among the tokens of one device (an aligned block of 128 tokens) no memory is named by more than 40 tokens, and in some such block a memory is named by exactly 40. `log_decay`: entries are negative.
All inputs are finite; a program needn't handle non-finite values.
Results may differ from a plain program's by a relative error of at most 0.015.
Values may be sent and summed in bfloat16 or wider, within the bound.
A program may use at most 128 MiB of HBM per device.

v0:
```python
import math

import jax
import jax.numpy as jnp
from jax import lax
from jax.sharding import Mesh
from jax.sharding import PartitionSpec as P

CTX = ("ctx_0", "ctx_1")
MEM = ("mem_0", "mem_1")


def filled_with(array, identity):
    return jax.tree.map(
        lambda part, zero: jnp.zeros_like(part) + jnp.asarray(zero, part.dtype), array, identity
    )


def carried_in(array, axes, combine, identity):
    before = start = filled_with(array, identity)
    running = array
    for axis in reversed(axes):
        devices, mine = (lax.axis_size(axis), lax.axis_index(axis))
        pieces = jax.tree.map(
            lambda part, kind: lax.all_gather(part.astype(kind), axis),
            running,
            (jnp.bfloat16, jnp.bfloat16),
        )
        inside, running = (start, start)
        for k in range(devices):
            passed = k < mine
            running = combine(
                running, jax.tree.map(lambda part, own: part[k].astype(own.dtype), pieces, array)
            )
            inside = jax.tree.map(lambda new, old: jnp.where(passed, new, old), running, inside)
        before = combine(inside, before)
    return before


def split_up(array, dim, devices):
    lengths = array.shape
    parts = array.reshape(*lengths[:dim], devices, lengths[dim] // devices, *lengths[dim + 1 :])
    return jnp.moveaxis(parts, dim, 0)


def in_order(parts, dim):
    parts = jnp.moveaxis(parts, 0, dim)
    lengths = parts.shape
    return parts.reshape(*lengths[:dim], lengths[dim] * lengths[dim + 1], *lengths[dim + 2 :])


def exchange_in_order(parts, axes, sequence):
    lengths = [lax.axis_size(a) for a in axes]
    parts = parts.reshape(*lengths, *parts.shape[1:])
    for k in sequence:
        parts = lax.all_to_all(parts, axes[k], split_axis=k, concat_axis=k, tiled=True)
    return parts.reshape(-1, *parts.shape[len(axes) :])


def core_and_chips(array, groups, sequence, split_dim, concat_dim):
    devices = lax.axis_size(groups[0]) * lax.axis_size(groups[1])
    parts = split_up(array, split_dim, devices)
    return in_order(exchange_in_order(parts, groups, sequence), concat_dim)


def split_parts(matrix):
    high = matrix.astype(jnp.bfloat16)
    low = (matrix - high.astype(jnp.float32)).astype(jnp.bfloat16)
    return (high, low)


def head_norm(rows):
    square_mean = jnp.mean(rows * rows, axis=-1, keepdims=True)
    return rows * lax.rsqrt(square_mean + 1e-06)


def local_terms(keys_in, incoming_values, rates_in):
    running_decay = jnp.cumsum(rates_in.astype(jnp.float32), axis=0)
    total = running_decay[-1]
    retained_mask = jnp.exp(total[None, :] - running_decay)
    upper_scaled_state, lower_scaled_state = split_parts(
        keys_in.astype(jnp.float32) * retained_mask[:, :, None]
    )
    state_increment = jnp.einsum(
        "dyn,dye->yne", upper_scaled_state, incoming_values, preferred_element_type=jnp.float32
    )
    state_increment = state_increment + jnp.einsum(
        "dyn,dye->yne", lower_scaled_state, incoming_values, preferred_element_type=jnp.float32
    )
    return (running_decay, jnp.exp(total), state_increment)


def compose_heads(earlier, later):
    return (earlier[0] * later[0], later[0][:, None, None] * earlier[1] + later[1])


def incoming_state(decay_total, state_increment):
    prior = carried_in(
        (decay_total, state_increment),
        CTX,
        compose_heads,
        (jnp.ones_like(decay_total), jnp.zeros_like(state_increment)),
    )
    return prior[1]


def memory_readout(
    queries_in, keys_in, incoming_values, running_decay, entering_state, query_scale
):
    count_rows = queries_in.shape[0]
    heads = queries_in.shape[1]
    hdim = queries_in.shape[2]
    width = math.gcd(heads, 8)
    causal = jnp.arange(count_rows)[:, None] >= jnp.arange(count_rows)[None, :]

    def one_group(index, result):
        start = index * width
        query_group_rows = lax.dynamic_slice_in_dim(queries_in, start, width, 1)
        group_key = lax.dynamic_slice_in_dim(keys_in, start, width, 1)
        group_value = lax.dynamic_slice_in_dim(incoming_values, start, width, 1)
        group_cumul = lax.dynamic_slice_in_dim(running_decay, start, width, 1)
        group_state = lax.dynamic_slice_in_dim(entering_state, start, width, 0)
        head_cumul = group_cumul.T
        masked = jnp.where(causal, head_cumul[:, :, None] - head_cumul[:, None, :], -jnp.inf)
        scores = jnp.einsum(
            "ihd,jhd->hij", query_group_rows, group_key, preferred_element_type=jnp.float32
        )
        weights = (jnp.exp(masked) * scores * query_scale).astype(jnp.bfloat16)
        intra = jnp.einsum("hij,jhd->ihd", weights, group_value, preferred_element_type=jnp.float32)
        upper_state_part, lower_state_part = split_parts(group_state)
        across_block_output = jnp.einsum(
            "epm,pmx->epx", query_group_rows, upper_state_part, preferred_element_type=jnp.float32
        )
        across_block_output = across_block_output + jnp.einsum(
            "epm,pmx->epx", query_group_rows, lower_state_part, preferred_element_type=jnp.float32
        )
        across_block_output = across_block_output * (jnp.exp(group_cumul) * query_scale)[:, :, None]
        group_out = (intra + across_block_output).astype(jnp.bfloat16)
        return lax.dynamic_update_slice_in_dim(result, group_out, start, 1)

    return lax.fori_loop(
        0, heads // width, one_group, jnp.zeros((count_rows, heads, hdim), jnp.bfloat16)
    )


def shards(queries, keys, values, log_decay, routes, route_weight, gain):
    tokens_here = queries.shape[1]
    heads = queries.shape[2]
    hdim = queries.shape[3]
    memories = lax.axis_size(MEM)
    capacity = 2 * tokens_here // memories + tokens_here // 16
    query_scale = hdim ** (-0.5)
    local_routes = routes[0]
    member = jnp.any(
        local_routes[:, :, None] == jnp.arange(memories, dtype=jnp.int32)[None, None, :], axis=1
    )
    counted = member.astype(jnp.int32)
    rank = jnp.cumsum(counted, axis=0) - counted
    match = member[None, :, :] & (
        rank[None, :, :] == jnp.arange(capacity, dtype=jnp.int32)[:, None, None]
    )
    source = jnp.sum(
        jnp.where(match, jnp.arange(tokens_here, dtype=jnp.int32)[None, :, None], 0), axis=1
    ).T.reshape(-1)
    filled = jnp.any(match, axis=1).T.reshape(-1)

    def packed(table):
        shaped = filled.reshape((-1,) + (1,) * (table.ndim - 1))
        rows_out = jnp.where(shaped, table[source], jnp.zeros((), table.dtype))
        return rows_out.reshape((memories, capacity) + table.shape[1:])

    query_send = packed(queries[0])
    key_send = packed(keys[0])
    value_send = packed(values[0])
    rate_send = packed(log_decay[0])
    count_rows = memories * capacity
    key_got, value_got, rate_got = (
        lax.all_to_all(key_send, MEM, split_axis=0, concat_axis=0, tiled=True),
        lax.all_to_all(value_send, MEM, split_axis=0, concat_axis=0, tiled=True),
        lax.all_to_all(rate_send, MEM, split_axis=0, concat_axis=0, tiled=True),
    )
    running_decay, decay_total, state_increment = local_terms(
        key_got.reshape(count_rows, heads, hdim),
        value_got.reshape(count_rows, heads, hdim),
        rate_got.reshape(count_rows, heads),
    )
    entering_state = incoming_state(decay_total, state_increment)
    query_got = core_and_chips(query_send, ("mem_0", "mem_1"), (1, 0), 0, 0)
    readout = memory_readout(
        query_got.reshape(count_rows, heads, hdim),
        key_got.reshape(count_rows, heads, hdim),
        value_got.reshape(count_rows, heads, hdim),
        running_decay,
        entering_state,
        query_scale,
    )
    returned = lax.all_to_all(
        readout.reshape(memories, capacity, heads, hdim),
        MEM,
        split_axis=0,
        concat_axis=0,
        tiled=True,
    )
    flat = returned.reshape(count_rows, heads, hdim)
    picked_rank = jnp.take_along_axis(rank, local_routes, axis=1)
    slot_index = local_routes * capacity + picked_rank
    first_out = head_norm(flat[slot_index[:, 0]].astype(jnp.float32))
    second_out = head_norm(flat[slot_index[:, 1]].astype(jnp.float32))
    local_weight = route_weight[0]
    mixed = first_out * local_weight[:, 0, None, None] + second_out * local_weight[:, 1, None, None]
    return (mixed * gain.reshape(heads, hdim)).astype(jnp.bfloat16)[None]


def solution(mesh):
    finer = Mesh(mesh.devices.reshape(4, 2, 8, 4), ("mem_0", "mem_1", "ctx_0", "ctx_1"))
    return jax.shard_map(
        shards,
        mesh=finer,
        in_specs=(
            P(CTX, MEM, None, None),
            P(CTX, MEM, None, None),
            P(CTX, MEM, None, None),
            P(CTX, MEM, None),
            P(CTX, MEM, None),
            P(CTX, MEM, None),
            P(),
        ),
        out_specs=P(CTX, MEM, None, None),
        check_vma=False,
    )
```

profile of v0, /device:TPU:1, one launch (start us, length us, event | category | flops | bytes accessed | tf_op | source)
XLA Modules:
  0.0 368.6 jit_solution(15745402740635472976)
XLA Ops:
  12.8 6.5 %all-to-all-start.1 = ((bf16[8,2,640]{2,1,0:T(2,128)(2,1)}), bf16[8,2,640]{2,1,0:T(2,128)(2,1)S(1)}, u32[]{:S(2)}, u32[]{:S(2)}) async-start(bf16[8,2,640]{2,1,0:T(2,128)(2,1)} %reshape.474), calls=%async_computation.1 | async-start | bytes 40960 | tf_op jit(solution)/shard_map/all_to_all | solution.py:180
  22.3 3.0 gather_fusion
  25.3 3.9 %broadcast_select_fusion.1 = (bf16[8,40,32,128]{3,2,1,0:T(8,128)(2,1)S(1)}, bf16[8,40,32,128]{3,2,1,0:T(8,128)(2,1)}) fusion(bf16[8,40,32,128]{3,2,1,0:T(8,128)(2,1)} %bitcast.233, pred[8,40]{1,0:T(8,128)(4,1)S(1)} %copy.76, bf16[8,40,32,128]{3,2,1,0:T(8,128)(2,1)} %bitcast.234), kind=kLoop, calls=%fused_computation.54 | loop fusion | flops 2621440 | bytes 10486080 | tf_op jit(solution)/shard_map/jit(_where)/select_n | solution.py:169
  31.7 4.8 %all-to-all-start.4 = ((bf16[8,40,32,128]{3,1,2,0:T(8,128)(2,1)}), bf16[8,40,32,128]{3,1,2,0:T(8,128)(2,1)}, u32[]{:S(2)}, u32[]{:S(2)}) async-start(bf16[8,40,32,128]{3,1,2,0:T(8,128)(2,1)} %copy.90), calls=%async_computation.4 | async-start | bytes 5242880 | tf_op jit(solution)/shard_map/all_to_all | solution.py:178
  36.5 4.3 %copy.78 = bf16[8,40,32,128]{3,1,2,0:T(8,128)(2,1)} copy(bf16[8,40,32,128]{3,2,1,0:T(8,128)(2,1)} %get-tuple-element.214) | data formatting | bytes 5242880 | tf_op jit(solution)/shard_map/jit(_where)/select_n | solution.py:169
  40.8 27.8 %all-to-all-done.4 = bf16[8,40,32,128]{3,1,2,0:T(8,128)(2,1)} async-done(((bf16[8,40,32,128]{3,1,2,0:T(8,128)(2,1)}), bf16[8,40,32,128]{3,1,2,0:T(8,128)(2,1)}, u32[]{:S(2)}, u32[]{:S(2)}) %all-to-all-start.4) | async-done | bytes 2621472 | tf_op jit(solution)/shard_map/all_to_all | solution.py:178
  68.6 5.1 %all-to-all-start = ((bf16[8,40,32,128]{3,1,2,0:T(8,128)(2,1)}), bf16[8,40,32,128]{3,1,2,0:T(8,128)(2,1)}, u32[]{:S(2)}, u32[]{:S(2)}) async-start(bf16[8,40,32,128]{3,1,2,0:T(8,128)(2,1)} %copy.78), calls=%async_computation | async-start | bytes 5242880 | tf_op jit(solution)/shard_map/all_to_all | solution.py:179
  79.4 3.8 %fusion.20 = (bf16[320,32,128]{2,1,0:T(8,128)(2,1)}, bf16[320,32,128]{2,1,0:T(8,128)(2,1)}) fusion(f32[320,32]{1,0:T(8,128)S(1)} %copy.92, bf16[8,40,32,128]{3,2,1,0:T(8,128)(2,1)S(1)} %copy.91), kind=kLoop, calls=%fused_computation.36 | loop fusion | flops 7864320 | bytes 7905280 | tf_op jit(solution)/shard_map/convert_element_type | solution.py:67
  83.2 22.6 %all-to-all-done = bf16[8,40,32,128]{3,1,2,0:T(8,128)(2,1)} async-done(((bf16[8,40,32,128]{3,1,2,0:T(8,128)(2,1)}), bf16[8,40,32,128]{3,1,2,0:T(8,128)(2,1)}, u32[]{:S(2)}, u32[]{:S(2)}) %all-to-all-start) | async-done | bytes 2621472 | tf_op jit(solution)/shard_map/all_to_all | solution.py:179
  111.1 3.5 add_convert_fusion
  114.9 7.1 %all-gather.1 = bf16[4,1,32]{2,1,0:T(2,128)(2,1)S(1)} all-gather(bf16[1,1,32]{2,1,0:T(2,128)(2,1)S(1)} %bitcast.245), channel_id=1, replica_groups=mesh['mem_0'=4,'mem_1'=2,'ctx_0'=8,'ctx_1'=4] {'ctx_1'}, dimensions={0}, use_global_device_ids=true | all-gather | bytes 320 | tf_op jit(solution)/shard_map/all_gather | solution.py:25
  122.1 44.2 %all-gather.8.cloned.1.call-done = bf16[128,128,128]{2,1,0:T(8,128)(2,1)} async-done(((bf16[32,128,128]{2,1,0:T(8,128)(2,1)}), bf16[128,128,128]{2,1,0:T(8,128)(2,1)}) %all-gather.8.cloned.1.call-update) | async-done | bytes 4194320 | tf_op jit(solution)/shard_map/all_gather | solution.py:25
  166.2 4.2 %fusion.47 = bf16[1,32,128,128]{3,2,1,0:T(8,128)(2,1)} fusion(f32[32]{0:T(128)S(1)} %get-tuple-element.207, f32[32]{0:T(128)S(1)} %get-tuple-element.209, f32[32]{0:T(128)S(1)} %get-tuple-element.210, f32[32]{0:T(128)S(1)} %get-tuple-element.208, bf16[128,128,128]{2,1,0:T(8,128)(2,1)} %all-gather.8.cloned.1.call-done), kind=kLoop, calls=%fused_computation.78 | loop fusion | flops 6291456 | bytes 5243392 | tf_op jit(solution)/shard_map/convert_element_type | solution.py:25
  176.5 6.1 %all_to_all.30 = bf16[4,2,1,40,32,128]{5,3,0,4,2,1:T(8,128)(2,1)S(1)} all-to-all(bf16[4,2,1,40,32,128]{5,3,0,4,2,1:T(8,128)(2,1)S(1)} %copy.87), channel_id=1, replica_groups=mesh['mem_0'=4,'mem_1'=2,'ctx_0'=8,'ctx_1'=4] {'mem_1'}, dimensions={1} | all-to-all | bytes 5242880 | tf_op jit(solution)/shard_map/all_to_all | solution.py:56
  184.6 4.5 %all-to-all-start.3 = ((bf16[4,2,1,40,32,128]{5,3,1,4,2,0:T(8,128)(2,1)}), bf16[4,2,1,40,32,128]{5,3,1,4,2,0:T(8,128)(2,1)}, u32[]{:S(2)}, u32[]{:S(2)}) async-start(bf16[4,2,1,40,32,128]{5,3,1,4,2,0:T(8,128)(2,1)} %copy.88), calls=%async_computation.3 | async-start | bytes 5242880 | tf_op jit(solution)/shard_map/all_to_all | solution.py:56
  189.1 14.6 %all-gather.2 = bf16[8,1,32]{2,1,0:T(2,128)(2,1)S(1)} all-gather(bf16[1,1,32]{2,1,0:T(2,128)(2,1)S(1)} %fusion.80), channel_id=1, replica_groups=mesh['mem_0'=4,'mem_1'=2,'ctx_0'=8,'ctx_1'=4] {'ctx_0'}, dimensions={0}, use_global_device_ids=true | all-gather | bytes 576 | tf_op jit(solution)/shard_map/all_gather | solution.py:25
  203.7 17.2 %all-to-all-done.3 = bf16[4,2,1,40,32,128]{5,3,1,4,2,0:T(8,128)(2,1)} async-done(((bf16[4,2,1,40,32,128]{5,3,1,4,2,0:T(8,128)(2,1)}), bf16[4,2,1,40,32,128]{5,3,1,4,2,0:T(8,128)(2,1)}, u32[]{:S(2)}, u32[]{:S(2)}) %all-to-all-start.3) | async-done | bytes 2621472 | tf_op jit(solution)/shard_map/all_to_all | solution.py:56
  220.9 3.9 %copy.89 = bf16[4,2,1,40,32,128]{5,4,3,1,0,2:T(8,128)(2,1)} copy(bf16[4,2,1,40,32,128]{5,3,1,4,2,0:T(8,128)(2,1)} %all-to-all-done.3) | data formatting | bytes 5242880 | tf_op jit(solution)/shard_map/all_to_all | solution.py:56
  224.8 40.4 %all-gather.6.cloned.1.call-done = bf16[8,32,128,128]{3,2,1,0:T(8,128)(2,1)} async-done(((bf16[1,32,128,128]{3,2,1,0:T(8,128)(2,1)}), bf16[8,32,128,128]{3,2,1,0:T(8,128)(2,1)}) %all-gather.6.cloned.1.call-update) | async-done | bytes 8388624 | tf_op jit(solution)/shard_map/all_gather | solution.py:25
  265.2 11.4 %fusion.30 = f32[32,128,128]{2,1,0:T(8,128)} fusion(bf16[8,32,128,128]{3,2,1,0:T(8,128)(2,1)} %all-gather.6.cloned.1.call-done, f32[32]{0:T(128)S(1)} %get-tuple-element.207, f32[32]{0:T(128)S(1)} %get-tuple-element.209, f32[32]{0:T(128)S(1)} %get-tuple-element.210, f32[32]{0:T(128)S(1)} %get-tuple-element.208, f32[32]{0:T(128)S(1)} %fusion.71, ...), kind=kLoop, calls=%fused_computation.61 | loop fusion | flops 25165824 | bytes 14681740 | tf_op jit(solution)/shard_map/add | solution.py:94
  278.7 31.9 %while.14 = (s32[]{:T(128)}, bf16[320,32,128]{2,0,1:T(8,128)(2,1)}, bf16[320,32,128]{2,0,1:T(8,128)(2,1)}, f32[320,32]{0,1:T(8,128)S(1)}, bf16[320,32,128]{2,1,0...) while((s32[]{:T(128)}, bf16[320,32,128]{2,0,1:T(8,128)(2,1)}, ...), condition=%wide.region_7.8_spmd.clone, body=%wide.region_6.7_spmd.clone.sunk | while | flops 593238528 | bytes 12874923 | solution.py:141
  310.6 5.0 %copy.97 = bf16[8,40,32,128]{3,2,1,0:T(8,128)(2,1)} copy(bf16[8,40,32,128]{3,1,0,2:T(8,128)(2,1)} %bitcast.231) | data formatting | bytes 5242880 | tf_op jit(solution)/shard_map/reshape | solution.py:198
  315.5 5.1 %all-to-all-start.5 = ((bf16[8,40,32,128]{3,2,1,0:T(8,128)(2,1)}), bf16[8,40,32,128]{3,2,1,0:T(8,128)(2,1)}, u32[]{:S(2)}, u32[]{:S(2)}) async-start(bf16[8,40,32,128]{3,2,1,0:T(8,128)(2,1)} %copy.97), calls=%async_computation.5 | async-start | bytes 5242880 | tf_op jit(solution)/shard_map/all_to_all | solution.py:197
  323.2 29.4 %all-to-all-done.5 = bf16[8,40,32,128]{3,2,1,0:T(8,128)(2,1)} async-done(((bf16[8,40,32,128]{3,2,1,0:T(8,128)(2,1)}), bf16[8,40,32,128]{3,2,1,0:T(8,128)(2,1)}, u32[]{:S(2)}, u32[]{:S(2)}) %all-to-all-start.5) | async-done | bytes 2621472 | tf_op jit(solution)/shard_map/all_to_all | solution.py:197
  (115 shorter events, 76.3 us)
Async XLA Ops:
  6.5 12.7 %copy-start = (bf16[1,128,32,128]{3,2,1,0:T(8,128)(2,1)S(1)}, bf16[1,128,32,128]{3,2,1,0:T(8,128)(2,1)}, u32[]{:S(2)}) copy-start(bf16[1,128,32,128]{3,2,1,0:T(8,128)(2,1)} %param.10) | copy-start | bytes 3145732
  12.8 19.0 %all-to-all-start.1 = ((bf16[8,2,640]{2,1,0:T(2,128)(2,1)}), bf16[8,2,640]{2,1,0:T(2,128)(2,1)S(1)}, u32[]{:S(2)}, u32[]{:S(2)}) async-start(bf16[8,2,640]{2,1,0:T(2,128)(2,1)} %reshape.474), calls=%async_computation.1 | async-start | bytes 40960 | tf_op jit(solution)/shard_map/all_to_all | solution.py:180
  19.2 3.0 copy-start.6
  31.7 36.9 %all-to-all-start.4 = ((bf16[8,40,32,128]{3,1,2,0:T(8,128)(2,1)}), bf16[8,40,32,128]{3,1,2,0:T(8,128)(2,1)}, u32[]{:S(2)}, u32[]{:S(2)}) async-start(bf16[8,40,32,128]{3,1,2,0:T(8,128)(2,1)} %copy.90), calls=%async_computation.4 | async-start | bytes 5242880 | tf_op jit(solution)/shard_map/all_to_all | solution.py:178
  68.6 37.2 %all-to-all-start = ((bf16[8,40,32,128]{3,1,2,0:T(8,128)(2,1)}), bf16[8,40,32,128]{3,1,2,0:T(8,128)(2,1)}, u32[]{:S(2)}, u32[]{:S(2)}) async-start(bf16[8,40,32,128]{3,1,2,0:T(8,128)(2,1)} %copy.78), calls=%async_computation | async-start | bytes 5242880 | tf_op jit(solution)/shard_map/all_to_all | solution.py:179
  73.7 92.5 %all-gather.8.cloned.1.call-start = ((), (), s32[]{:S(2)}) async-start(), calls=%async_computation.7 | async-start | bytes 5242880 | tf_op jit(solution)/shard_map/all_gather | solution.py:25
  77.9 1.5 copy-start.2
  105.8 2.6 copy-start.4
  108.4 2.6 copy-start.3
  108.5 2.7 copy-start.5
  114.7 150.5 %all-gather.6.cloned.1.call-start = ((), (), s32[]{:S(2)}) async-start(), calls=%async_computation.6 | async-start | bytes 9437184 | tf_op jit(solution)/shard_map/all_gather | solution.py:25
  166.2 4.3 %copy-start.7 = (bf16[1,128,32,128]{3,2,1,0:T(8,128)(2,1)S(1)}, bf16[1,128,32,128]{3,2,1,0:T(8,128)(2,1)}, u32[]{:S(2)}) copy-start(bf16[1,128,32,128]{3,2,1,0:T(8,128)(2,1)} %param.9) | copy-start | bytes 3145732
  184.6 36.3 %all-to-all-start.3 = ((bf16[4,2,1,40,32,128]{5,3,1,4,2,0:T(8,128)(2,1)}), bf16[4,2,1,40,32,128]{5,3,1,4,2,0:T(8,128)(2,1)}, u32[]{:S(2)}, u32[]{:S(2)}) async-start(bf16[4,2,1,40,32,128]{5,3,1,4,2,0:T(8,128)(2,1)} %copy.88), calls=%async_computation.3 | async-start | bytes 5242880 | tf_op jit(solution)/shard_map/all_to_all | solution.py:56
  315.5 5.1 %copy-start.9 = (s32[1,128,2]{1,2,0:T(2,128)S(1)}, s32[1,128,2]{1,2,0:T(2,128)}, u32[]{:S(2)}) copy-start(s32[1,128,2]{1,2,0:T(2,128)} %param.13) | copy-start | bytes 3076
  315.5 37.1 %all-to-all-start.5 = ((bf16[8,40,32,128]{3,2,1,0:T(8,128)(2,1)}), bf16[8,40,32,128]{3,2,1,0:T(8,128)(2,1)}, u32[]{:S(2)}, u32[]{:S(2)}) async-start(bf16[8,40,32,128]{3,2,1,0:T(8,128)(2,1)} %copy.97), calls=%async_computation.5 | async-start | bytes 5242880 | tf_op jit(solution)/shard_map/all_to_all | solution.py:197
  320.9 2.3 copy-start.10
  355.2 3.9 %copy-start.8 = (f32[4096]{0:T(1024)S(1)}, f32[4096]{0:T(1024)}, u32[]{:S(2)}) copy-start(f32[4096]{0:T(1024)} %param.15) | copy-start | bytes 49156
  355.8 5.9 %copy-start.1 = (bf16[1,128,32,128]{3,2,1,0:T(8,128)(2,1)S(1)}, bf16[1,128,32,128]{3,2,1,0:T(8,128)(2,1)}, u32[]{:S(2)}) copy-start(bf16[1,128,32,128]{3,2,1,0:T(8,128)(2,1)} %param.10) | copy-start | bytes 3145732
Sparse Core Ops, SparseCore 0:
  114.8 51.3 all-gather.7
  170.6 94.5 all-gather.5
where the time goes:
time: 370 us; the launch traced here: 369 us
  waiting for transfers between devices  182 us (49%)
  local copies, waits for them, and re-layouts  54.3 us (15%)
  other arithmetic  32.7 us (9%)
  matrix products  32.2 us (9%)
  blocking collectives  27.8 us (8%)
  starting transfers between devices  26.1 us (7%)
  between operations  13.8 us (4%)
    all_gather x2, waiting for transfers between devices, carried_in(): lax.all_gather(part.astype(kind), axis)  84.6 us
    all_to_all x1, waiting for transfers between devices, shards(): lax.all_to_all(readout.reshape(memories, capacity, heads, hdim), MEM, spl...  29.4 us
    all_to_all x1, waiting for transfers between devices, shards(): lax.all_to_all(key_send, MEM, split_axis=0, concat_axis=0, tiled=True)  27.8 us
    all_to_all x1, waiting for transfers between devices, shards(): lax.all_to_all(value_send, MEM, split_axis=0, concat_axis=0, tiled=True)  22.6 us
    all_gather x2, blocking collectives, carried_in(): lax.all_gather(part.astype(kind), axis)  21.7 us
    all_to_all x1, waiting for transfers between devices, exchange_in_order(): lax.all_to_all(parts, axes[k], split_axis=k, concat_axis=k, tiled=True)  17.2 us
    add x1, other arithmetic, compose_heads(): later[0][:, None, None] * earlier[1] + later[1]  11.4 us
    dot_general x4, matrix products, one_group(): jnp.einsum('hij,jhd->ihd', weights, group_value, preferred_element_type=j...  11 us
  transfers between devices with their start and end apart: 7, of which 6 were waited for; matrix products, arithmetic and copies ran while one was open for 11% of the time, Pallas kernels for 0%

commit v1 on v0

v1 whole, which is shorter than its diff:
```python
import functools

import jax
import jax.numpy as jnp
from jax import lax
from jax.experimental import pallas as pl
from jax.experimental.pallas import tpu as pltpu
from jax.sharding import Mesh
from jax.sharding import PartitionSpec as P

GROUP = ("ctx_1", "mem_0", "mem_1")
SCAN = "ctx_0"
HEADS = 32
HD = 128
TOK = 128
MEM = 8
META = 16
PAIR = 2 * TOK
TILES = HEADS // 2
BF = jnp.bfloat16
F32 = jnp.float32
LIMIT = 56 * 1024 * 1024


def dot(a, b):
    return jnp.dot(a, b, preferred_element_type=F32)


def vmem_call(kernel, outs, scratch=()):
    return pl.pallas_call(
        kernel,
        out_shape=outs,
        scratch_shapes=list(scratch),
        compiler_params=pltpu.CompilerParams(vmem_limit_bytes=LIMIT),
    )


def pack_kernel(q_ref, k_ref, v_ref, meta_ref, qt_ref, kp_ref, vt_ref, flat):
    for source, dest, turned in ((k_ref, kp_ref, False), (v_ref, vt_ref, True), (q_ref, qt_ref, True)):
        flat[...] = source[...].astype(F32).reshape(TOK * HEADS, HD)

        def one(h, _):
            slab = flat[pl.ds(h, TOK, stride=HEADS), :]
            if turned:
                slab = slab.T
            dest[h, 0:TOK, :] = slab.astype(BF)
            return 0

        lax.fori_loop(0, HEADS, one, 0)
    kp_ref[:, TOK:, :] = meta_ref[...]


def pack(q, k, v, meta):
    slab = jax.ShapeDtypeStruct((HEADS, TOK, HD), BF)
    return vmem_call(
        pack_kernel,
        (slab, jax.ShapeDtypeStruct((HEADS, TOK + META, HD), BF), slab),
        [pltpu.VMEM((TOK * HEADS, HD), F32)],
    )(q, k, v, meta)


def unpack_kernel(got_ref, out_ref, flat):
    def one(h, _):
        flat[pl.ds(h, TOK, stride=HEADS), :] = got_ref[h].astype(F32)
        return 0

    lax.fori_loop(0, HEADS, one, 0)
    out_ref[...] = flat[...].astype(BF).reshape(TOK, HEADS, HD)


def unpack(got):
    return vmem_call(
        unpack_kernel,
        jax.ShapeDtypeStruct((TOK, HEADS, HD), BF),
        [pltpu.VMEM((TOK * HEADS, HD), F32)],
    )(got)


def tile_meta(kp_ref, c):
    first = kp_ref[2 * c, TOK : TOK + META, :].astype(F32)
    second = kp_ref[2 * c + 1, TOK : TOK + META, :].astype(F32)
    return jnp.concatenate([first, second], axis=1)


def tile_masks(meta):
    ids = lax.broadcasted_iota(jnp.int32, (MEM, PAIR), 0).astype(F32)
    oh0 = jnp.where(meta[1:2, :] == ids, 1.0, 0.0)
    oh1 = jnp.where(meta[2:3, :] == ids, 1.0, 0.0)
    return oh0, oh1


def running_decays(kp_ref, rates, sums):
    def one(c, _):
        meta = tile_meta(kp_ref, c)
        oh0, oh1 = tile_masks(meta)
        rates[pl.ds(c * MEM, MEM), :] = (oh0 + oh1) * meta[0:1, :]
        return 0

    lax.fori_loop(0, TILES, one, 0)
    before = lax.broadcasted_iota(jnp.int32, (PAIR, PAIR), 0)
    after = lax.broadcasted_iota(jnp.int32, (PAIR, PAIR), 1)
    upper = jnp.where(before <= after, 1.0, 0.0).astype(BF)
    sums[...] = dot(rates[...].astype(BF), upper)


def pair(ref, c):
    return jnp.concatenate([ref[2 * c], ref[2 * c + 1]], axis=1)


def pair_keys(kp_ref, c):
    return jnp.concatenate([kp_ref[2 * c, 0:TOK, :], kp_ref[2 * c + 1, 0:TOK, :]], axis=0)


def tile_increment(vt, keys, mask, run):
    total = run[:, PAIR - 1 : PAIR]
    kept = mask * jnp.exp(total - run)
    wide = vt.astype(F32)
    scaled = jnp.concatenate([(wide * kept[m : m + 1, :]).astype(BF) for m in range(MEM)], axis=0)
    return dot(scaled, keys)


def advance(state, inc, total):
    gone = jnp.exp(total)
    for m in range(MEM):
        cols = slice(m * HD, (m + 1) * HD)
        state[:, cols] = state[:, cols] * gone[m : m + 1, :] + inc[cols, :]


def state_kernel(kp_ref, vt_ref, out_ref, rates, sums, state):
    running_decays(kp_ref, rates, sums)
    state[...] = jnp.zeros_like(state)

    def one(c, whole):
        oh0, oh1 = tile_masks(tile_meta(kp_ref, c))
        run = sums[pl.ds(c * MEM, MEM), :]
        inc = tile_increment(pair(vt_ref, c), pair_keys(kp_ref, c), oh0 + oh1, run)
        total = run[:, PAIR - 1 : PAIR]
        advance(state, inc, total)
        return whole + total

    whole = lax.fori_loop(0, TILES, one, jnp.zeros((MEM, 1), F32))
    left = jnp.exp(whole)
    high = left.astype(BF).astype(F32)
    low = left - high
    row = lax.broadcasted_iota(jnp.int32, (META, HD), 0)
    for m in range(MEM):
        out_ref[m, 0:HD, :] = state[:, m * HD : (m + 1) * HD].astype(BF)
        out_ref[m, HD:, :] = jnp.where(row == 0, high[m : m + 1, :], low[m : m + 1, :]).astype(BF)


def tile_scratch():
    return [
        pltpu.VMEM((TILES * MEM, PAIR), F32),
        pltpu.VMEM((TILES * MEM, PAIR), F32),
        pltpu.VMEM((HD, MEM * HD), F32),
    ]


def chunk_state(kp, vt):
    return vmem_call(
        state_kernel, jax.ShapeDtypeStruct((MEM, HD + META, HD), BF), tile_scratch()
    )(kp, vt)


def compose_kernel(parts_ref, out_ref):
    run = jnp.zeros((HD, HD), F32)
    for z in range(parts_ref.shape[0]):
        out_ref[z] = run.astype(BF)
        left = parts_ref[z, HD : HD + META, :].astype(F32)
        run = run * (left[0:1, :] + left[1:2, :]) + parts_ref[z, 0:HD, :].astype(F32)


def compose(parts):
    return vmem_call(compose_kernel, jax.ShapeDtypeStruct((parts.shape[0], HD, HD), BF))(parts)


def split_rows(rows):
    high = rows.astype(BF).astype(F32)
    return high, rows - high


def read_kernel(kp_ref, vt_ref, qt_ref, enter_ref, gain_ref, out_ref, rates, sums, state):
    scale = HD**-0.5
    running_decays(kp_ref, rates, sums)
    for m in range(MEM):
        state[:, m * HD : (m + 1) * HD] = enter_ref[m].astype(F32)
    gain = gain_ref[...]
    earlier = lax.broadcasted_iota(jnp.int32, (PAIR, PAIR), 0)
    later = lax.broadcasted_iota(jnp.int32, (PAIR, PAIR), 1)
    causal = earlier <= later

    def one(c, _):
        meta = tile_meta(kp_ref, c)
        oh0, oh1 = tile_masks(meta)
        mask = oh0 + oh1
        run = sums[pl.ds(c * MEM, MEM), :]
        total = run[:, PAIR - 1 : PAIR]
        middle = 0.5 * total
        up = jnp.exp(run - middle) * scale
        down_h, down_l = split_rows(mask * jnp.exp(middle - run))
        below = jnp.concatenate([down_h, down_l, down_h, down_l], axis=0).astype(BF)
        vt, keys, qt = pair(vt_ref, c), pair_keys(kp_ref, c), pair(qt_ref, c)
        scores = dot(keys, qt)
        old = state[...].astype(BF)
        reach = jnp.exp(run) * scale
        mixed = jnp.zeros((HD, PAIR), F32)
        grouped = qt.reshape(HD // 16, 16, PAIR)
        for oh, high_row in ((oh0, 3), (oh1, 5)):
            up_h, up_l = split_rows(oh * up)
            above = jnp.concatenate([up_h, up_h, up_l, up_l], axis=0).astype(BF)
            decay = lax.dot_general(
                below, above, (((0,), (0,)), ((), ())), preferred_element_type=F32
            )
            weights = jnp.where(causal, scores * decay, 0.0).astype(BF)
            inside = dot(vt, weights)
            chosen = jnp.concatenate(
                [
                    (
                        grouped * jnp.broadcast_to(oh[m : m + 1, :], (16, PAIR)).astype(BF)[None]
                    ).reshape(HD, PAIR)
                    for m in range(MEM)
                ],
                axis=0,
            )
            across = dot(old, chosen)
            full = inside + across * jnp.sum(oh * reach, axis=0, keepdims=True)
            square = jnp.mean(full * full, axis=0, keepdims=True)
            weight = meta[high_row : high_row + 1, :] + meta[high_row + 1 : high_row + 2, :]
            mixed = mixed + full * (lax.rsqrt(square + 1e-06) * weight)
        mixed = (mixed * gain).T.astype(BF)
        out_ref[2 * c] = mixed[0:TOK]
        out_ref[2 * c + 1] = mixed[TOK:]
        advance(state, tile_increment(vt, keys, mask, run), total)
        return 0

    lax.fori_loop(0, TILES, one, 0)


def read(kp, vt, qt, enter, gain):
    return vmem_call(
        read_kernel, jax.ShapeDtypeStruct((HEADS, TOK, HD), BF), tile_scratch()
    )(kp, vt, qt, enter, gain)


def make_meta(log_decay, routes, route_weight):
    high = route_weight.astype(BF)
    low = (route_weight - high.astype(F32)).astype(BF)
    named = routes.astype(BF)
    common = jnp.stack([named[:, 0], named[:, 1], high[:, 0], low[:, 0], high[:, 1], low[:, 1]])
    common = jnp.pad(common, ((0, META - 7), (0, 0)))
    common = jnp.broadcast_to(common[None], (HEADS, META - 1, TOK))
    return jnp.concatenate([log_decay.T[:, None, :], common], axis=1)


def exchange(parts, axes):
    return lax.all_to_all(parts, axes, split_axis=0, concat_axis=0, tiled=True)


def shards(queries, keys, values, log_decay, routes, route_weight, gain):
    meta = make_meta(log_decay[0], routes[0], route_weight[0])
    qt, kp, vt = pack(queries[0], keys[0], values[0], meta)
    kp = exchange(kp, GROUP)
    vt = exchange(vt, GROUP)
    qt = exchange(qt, GROUP)
    mine = chunk_state(kp, vt)
    enter = exchange(compose(exchange(mine, SCAN)), SCAN)
    own = lax.dynamic_slice_in_dim(gain, lax.axis_index(GROUP) * HD, HD)[:, None]
    done = read(kp, vt, qt, enter, own)
    return unpack(exchange(done, GROUP))[None]


def solution(mesh):
    finer = Mesh(mesh.devices.reshape(4, 2, 8, 4), ("mem_0", "mem_1", "ctx_0", "ctx_1"))
    ctx = ("ctx_0", "ctx_1")
    mem = ("mem_0", "mem_1")
    return jax.shard_map(
        shards,
        mesh=finer,
        in_specs=(
            P(ctx, mem, None, None),
            P(ctx, mem, None, None),
            P(ctx, mem, None, None),
            P(ctx, mem, None),
            P(ctx, mem, None),
            P(ctx, mem, None),
            P(),
        ),
        out_specs=P(ctx, mem, None, None),
        check_vma=False,
    )
```

time: 370 us -> 179 us (0.48)
  waiting for transfers between devices: 182 us -> 26.7 us
  blocking collectives: 27.8 us -> 90.6 us
  local copies, waits for them, and re-layouts: 54.3 us -> 2.31 us
  Pallas kernels: 0 us -> 47.6 us
  matrix products: 32.2 us -> 0 us
  other arithmetic: 32.7 us -> 2.09 us
  starting transfers between devices: 26.1 us -> 8.43 us
  between operations: 13.8 us -> 0.06 us
    all_gather x2 -> x0, waiting for transfers between devices: 84.6 us -> none  [carried_in(): lax.all_gather(part.astype(kind), axis)]
    all_to_all x1 -> x4, blocking collectives: 6.14 us -> 90.6 us  [exchange(): return lax.all_to_all(parts, axes, split_axis=0, concat_axis=0, tiled=True)]
    all_to_all x5 -> x2, waiting for transfers between devices: 97 us -> 26.7 us  [exchange(): return lax.all_to_all(parts, axes, split_axis=0, concat_axis=0, tiled=True)]
    pallas_call x0 -> x5, Pallas kernels: none -> 47.6 us  [the longest x1 17.8 us: read(): vmem_call(read_kernel, jax.ShapeDtypeStruct((HEADS, TOK, HD), BF), tile_s...]
    dot_general x14 -> x0, matrix products: 32.2 us -> none  [the longest x4 11 us: one_group(): jnp.einsum('hij,jhd->ihd', weights, group_value, preferred_element_type=j...]
    all_gather x2 -> x0, blocking collectives: 21.7 us -> none  [carried_in(): lax.all_gather(part.astype(kind), axis)]
    gather x11 -> x0, local copies, waits for them, and re-layouts: 17.9 us -> none  [the longest x5 10.5 us: packed(): rows_out = jnp.where(shaped, table[source], jnp.zeros((), table.dtype))]
    all_to_all x5 -> x2, starting transfers between devices: 26.1 us -> 8.43 us  [exchange(): return lax.all_to_all(parts, axes, split_axis=0, concat_axis=0, tiled=True)]
  transfers between devices with their start and end apart: 7 -> 2, of which waited for: 6 -> 2; matrix products, arithmetic and copies ran while one was open for 11% -> 0% of each run, Pallas kernels for 0% -> 1%
where the time goes in v1:
time: 179 us; the launch traced here: 178 us
  blocking collectives  90.6 us (51%)
  Pallas kernels  47.6 us (27%)
  waiting for transfers between devices  26.7 us (15%)
  starting transfers between devices  8.43 us (5%)
  local copies, waits for them, and re-layouts  2.31 us (1%)
  other arithmetic  2.09 us (1%)
    all_to_all x4, blocking collectives, exchange(): return lax.all_to_all(parts, axes, split_axis=0, concat_axis=0, tiled=True)  90.6 us
    all_to_all x2, waiting for transfers between devices, exchange(): return lax.all_to_all(parts, axes, split_axis=0, concat_axis=0, tiled=True)  26.7 us
    pallas_call x1, Pallas kernels, read(): vmem_call(read_kernel, jax.ShapeDtypeStruct((HEADS, TOK, HD), BF), tile_s...  17.8 us
    pallas_call x1, Pallas kernels, pack(): vmem_call(pack_kernel, (slab, jax.ShapeDtypeStruct((HEADS, TOK + META, HD...  15.2 us
    pallas_call x1, Pallas kernels, chunk_state(): vmem_call(state_kernel, jax.ShapeDtypeStruct((MEM, HD + META, HD), BF), t...  8.51 us
    all_to_all x2, starting transfers between devices, exchange(): return lax.all_to_all(parts, axes, split_axis=0, concat_axis=0, tiled=True)  8.43 us
    pallas_call x1, Pallas kernels, unpack(): vmem_call(unpack_kernel, jax.ShapeDtypeStruct((TOK, HEADS, HD), BF), [plt...  4.44 us
  transfers between devices with their start and end apart: 2, of which 2 were waited for; matrix products, arithmetic and copies ran while one was open for 0% of the time, Pallas kernels for 1%

profile of v1, /device:TPU:1, one launch (start us, length us, event | category | flops | bytes accessed | tf_op | source)
XLA Modules:
  0.0 177.9 jit_solution(15930016750601622891)
XLA Ops:
  0.0 0.0 copy-start
  0.0 0.7 convert_bitcast_fusion
  0.7 0.7 fusion
  1.4 0.7 copy.9
  2.2 0.7 pad_maximum_fusion.meta_ref
  2.9 15.2 %shard_map.73 = (bf16[32,128,128]{2,1,0:T(8,128)(2,1)}, bf16[32,144,128]{2,1,0:T(8,128)(2,1)}, bf16[32,128,128]{2,1,0:T(8,128)(2,1)}) custom-call(bf16[128,32,128]{2,1,0:T(8,128)(2,1)} %bitcast.31, bf16[128,32,128]{2,1,0:T(8,128)(2,1)} %bitcast.32, bf16[128,32,128]{2,1,0:T(8,128)(2,1)} %bitcast.33, bf16[32,16,128]{2,1,0:T(8,128)(2,1)} %pad_maximum_fusion.meta_ref), custom_call_target="tpu_custom_call" | custom-call | tf_op jit(solution)/shard_map/pallas_call | solution.py:55
  18.1 25.7 %all_to_all.30.vt_ref = bf16[32,128,128]{2,1,0:T(8,128)(2,1)} all-to-all(bf16[32,128,128]{2,1,0:T(8,128)(2,1)} %get-tuple-element.9), channel_id=1, replica_groups=mesh['mem_0'=4,'mem_1'=2,'ctx_0'=8,'ctx_1'=4] {'ctx_1','mem_0','mem_1'}, dimensions={0} | all-to-all | bytes 2097152 | tf_op jit(solution)/shard_map/all_to_all | solution.py:256
  43.8 0.0 copy-done.2
  43.8 22.8 %all_to_all.31.kp_ref = bf16[32,144,128]{2,1,0:T(8,128)(2,1)} all-to-all(bf16[32,144,128]{2,1,0:T(8,128)(2,1)S(1)} %copy-done.2), channel_id=1, replica_groups=mesh['mem_0'=4,'mem_1'=2,'ctx_0'=8,'ctx_1'=4] {'ctx_1','mem_0','mem_1'}, dimensions={0} | all-to-all | bytes 2359296 | tf_op jit(solution)/shard_map/all_to_all | solution.py:256
  66.6 8.5 %shard_map.74 = bf16[8,144,128]{2,1,0:T(8,128)(2,1)} custom-call(bf16[32,144,128]{2,1,0:T(8,128)(2,1)} %all_to_all.31.kp_ref, bf16[32,128,128]{2,1,0:T(8,128)(2,1)} %all_to_all.30.vt_ref), custom_call_target="tpu_custom_call" | custom-call | tf_op jit(solution)/shard_map/pallas_call | solution.py:160
  75.1 20.4 %all_to_all.32.parts_ref = bf16[8,144,128]{2,1,0:T(8,128)(2,1)} all-to-all(bf16[8,144,128]{2,1,0:T(8,128)(2,1)} %shard_map.74), channel_id=1, replica_groups=mesh['mem_0'=4,'mem_1'=2,'ctx_0'=8,'ctx_1'=4] {'ctx_0'}, dimensions={0} | all-to-all | bytes 589824 | tf_op jit(solution)/shard_map/all_to_all | solution.py:256
  95.5 5.0 %all-to-all-start.2 = ((bf16[32,128,128]{2,1,0:T(8,128)(2,1)}), bf16[32,128,128]{2,1,0:T(8,128)(2,1)S(1)}, u32[]{:S(2)}, u32[]{:S(2)}) async-start(bf16[32,128,128]{2,1,0:T(8,128)(2,1)} %get-tuple-element.10), calls=%async_computation.2 | async-start | bytes 2097152 | tf_op jit(solution)/shard_map/all_to_all | solution.py:256
  100.5 1.7 shard_map.75
  102.2 15.3 %all-to-all-done.2.qt_ref = bf16[32,128,128]{2,1,0:T(8,128)(2,1)S(1)} async-done(((bf16[32,128,128]{2,1,0:T(8,128)(2,1)}), bf16[32,128,128]{2,1,0:T(8,128)(2,1)S(1)}, u32[]{:S(2)}, u32[]{:S(2)}) %all-to-all-start.2) | async-done | bytes 1048608 | tf_op jit(solution)/shard_map/all_to_all | solution.py:256
  117.5 3.4 %all-to-all-start.4 = ((bf16[8,128,128]{2,1,0:T(8,128)(2,1)}), bf16[8,128,128]{2,1,0:T(8,128)(2,1)S(1)}, u32[]{:S(2)}, u32[]{:S(2)}) async-start(bf16[8,128,128]{2,1,0:T(8,128)(2,1)} %shard_map.75), calls=%async_computation.4 | async-start | bytes 524288 | tf_op jit(solution)/shard_map/all_to_all | solution.py:256
  120.9 0.0 copy-done
  120.9 0.1 dynamic-slice_bitcast_fusion
  121.0 0.7 copy.10.gain_ref
  121.7 11.5 %all-to-all-done.4.enter_ref = bf16[8,128,128]{2,1,0:T(8,128)(2,1)S(1)} async-done(((bf16[8,128,128]{2,1,0:T(8,128)(2,1)}), bf16[8,128,128]{2,1,0:T(8,128)(2,1)S(1)}, u32[]{:S(2)}, u32[]{:S(2)}) %all-to-all-start.4) | async-done | bytes 262176 | tf_op jit(solution)/shard_map/all_to_all | solution.py:256
  133.2 0.0 copy-done.1
  133.2 0.7 copy-done.3
  133.9 17.8 %shard_map.76 = bf16[32,128,128]{2,1,0:T(8,128)(2,1)} custom-call(bf16[32,144,128]{2,1,0:T(8,128)(2,1)} %all_to_all.31.kp_ref, bf16[32,128,128]{2,1,0:T(8,128)(2,1)} %all_to_all.30.vt_ref, bf16[32,128,128]{2,1,0:T(8,128)(2,1)} %copy-done.1, bf16[8,128,128]{2,1,0:T(8,128)(2,1)} %copy-done.3, f32[128,1]{1,0:T(8,128)} %copy.10.gain_ref), custom_call_target="tpu_custom_call" | custom-call | tf_op jit(solution)/shard_map/pallas_call | solution.py:240
  151.7 21.7 %all_to_all.33.got_ref = bf16[32,128,128]{2,1,0:T(8,128)(2,1)} all-to-all(bf16[32,128,128]{2,1,0:T(8,128)(2,1)} %shard_map.76), channel_id=1, replica_groups=mesh['mem_0'=4,'mem_1'=2,'ctx_0'=8,'ctx_1'=4] {'ctx_1','mem_0','mem_1'}, dimensions={0} | all-to-all | bytes 2097152 | tf_op jit(solution)/shard_map/all_to_all | solution.py:256
  173.4 4.4 %shard_map.77 = bf16[128,32,128]{2,1,0:T(8,128)(2,1)} custom-call(bf16[32,128,128]{2,1,0:T(8,128)(2,1)} %all_to_all.33.got_ref), custom_call_target="tpu_custom_call" | custom-call | tf_op jit(solution)/shard_map/pallas_call | solution.py:72
  (8 shorter events, 0.1 us)
Async XLA Ops:
  0.0 120.9 %copy-start = (f32[4096]{0:T(1024)S(1)}, f32[4096]{0:T(1024)}, u32[]{:S(2)}) copy-start(f32[4096]{0:T(1024)} %param.13) | copy-start | bytes 49156
  18.1 25.7 %copy-start.2 = (bf16[32,144,128]{2,1,0:T(8,128)(2,1)S(1)}, bf16[32,144,128]{2,1,0:T(8,128)(2,1)}, u32[]{:S(2)}) copy-start(bf16[32,144,128]{2,1,0:T(8,128)(2,1)} %get-tuple-element.8) | copy-start | bytes 3538948
  95.5 22.0 %all-to-all-start.2 = ((bf16[32,128,128]{2,1,0:T(8,128)(2,1)}), bf16[32,128,128]{2,1,0:T(8,128)(2,1)S(1)}, u32[]{:S(2)}, u32[]{:S(2)}) async-start(bf16[32,128,128]{2,1,0:T(8,128)(2,1)} %get-tuple-element.10), calls=%async_computation.2 | async-start | bytes 2097152 | tf_op jit(solution)/shard_map/all_to_all | solution.py:256
  117.5 15.7 %copy-start.1 = (bf16[32,128,128]{2,1,0:T(8,128)(2,1)}, bf16[32,128,128]{2,1,0:T(8,128)(2,1)S(1)}, u32[]{:S(2)}) copy-start(bf16[32,128,128]{2,1,0:T(8,128)(2,1)S(1)} %all-to-all-done.2.qt_ref) | copy-start | bytes 3145732
  117.5 15.7 %all-to-all-start.4 = ((bf16[8,128,128]{2,1,0:T(8,128)(2,1)}), bf16[8,128,128]{2,1,0:T(8,128)(2,1)S(1)}, u32[]{:S(2)}, u32[]{:S(2)}) async-start(bf16[8,128,128]{2,1,0:T(8,128)(2,1)} %shard_map.75), calls=%async_computation.4 | async-start | bytes 524288 | tf_op jit(solution)/shard_map/all_to_all | solution.py:256
  133.2 0.7 copy-start.3

commit v2 on v1

v2 whole, which is shorter than its diff:
```python
import jax
import jax.numpy as jnp
from jax import lax
from jax.experimental import pallas as pl
from jax.experimental.pallas import tpu as pltpu
from jax.sharding import Mesh
from jax.sharding import PartitionSpec as P

HEADS = 32
HD = 128
TOK = 128
MEM = 8
META = 16
PAIR = 2 * TOK
TILES = HEADS // 2
SLAB = TOK + META + HD
BF = jnp.bfloat16
F32 = jnp.float32
SCALE = HD**-0.5
MESH = pl.DeviceIdType.MESH


def dot(a, b):
    return jnp.dot(a, b, preferred_element_type=F32)


class Place:
    def __init__(self):
        self.x, self.y = lax.axis_index("ctx_1"), lax.axis_index("mem_0")
        self.c, self.z = lax.axis_index("mem_1"), lax.axis_index("ctx_0")
        self.me = (self.x * 4 + self.y) * 2 + self.c

    def target(self, chip, core):
        x, y = lax.rem(self.x + chip // 4, 4), lax.rem(self.y + lax.rem(chip, 4), 4)
        c = lax.rem(self.c + core, 2)
        return x * 4 + y, (x * 4 + y) * 2 + c, {"ctx_1": x, "mem_0": y, "mem_1": c}

    def source(self, chip, core):
        x = lax.rem(self.x + 4 - chip // 4, 4)
        y = lax.rem(self.y + 4 - lax.rem(chip, 4), 4)
        c = lax.rem(self.c + core, 2)
        return x * 4 + y, (x * 4 + y) * 2 + c

    def along(self, off):
        to = lax.rem(self.z + off, 8)
        return to, {"ctx_0": to}

    def back(self, off):
        return lax.rem(self.z + 8 - off, 8)


def remote(src, dst, sems, slot, device):
    return pltpu.make_async_remote_copy(
        src_ref=src,
        dst_ref=dst,
        send_sem=sems[0].at[slot],
        recv_sem=sems[1].at[slot],
        device_id=device,
        device_id_type=MESH,
    )


def loop(lo, hi, body):
    def step(i, _):
        body(i)
        return 0

    lax.fori_loop(lo, hi, step, 0)


def tile_meta(got, c):
    first = got[2 * c, TOK : TOK + META, :].astype(F32)
    second = got[2 * c + 1, TOK : TOK + META, :].astype(F32)
    return jnp.concatenate([first, second], axis=1)


def tile_masks(meta):
    ids = lax.broadcasted_iota(jnp.int32, (MEM, PAIR), 0).astype(F32)
    return jnp.where(meta[1:2, :] == ids, 1.0, 0.0), jnp.where(meta[2:3, :] == ids, 1.0, 0.0)


def pair_keys(got, c):
    return jnp.concatenate([got[2 * c, 0:TOK, :], got[2 * c + 1, 0:TOK, :]], axis=0)


def pair_values(got, c):
    return jnp.concatenate([got[2 * c, TOK + META :, :], got[2 * c + 1, TOK + META :, :]], axis=1)


def split_rows(rows):
    high = rows.astype(BF).astype(F32)
    return high, rows - high


def chosen_queries(qt, oh):
    grouped = qt.reshape(HD // 16, 16, PAIR)
    parts = []
    for m in range(MEM):
        row = jnp.broadcast_to(oh[m : m + 1, :], (16, PAIR)).astype(BF)
        parts.append((grouped * row[None]).reshape(HD, PAIR))
    return jnp.concatenate(parts, axis=0)


def layer_kernel(
    q_ref,
    k_ref,
    v_ref,
    rate_ref,
    route_ref,
    weight_ref,
    gain_ref,
    out_ref,
    flat_a,
    flat_b,
    rates,
    slabs,
    got,
    q_out,
    q_got,
    o_out,
    o_got,
    z_out,
    z_got,
    e_out,
    e_got,
    enter,
    sums,
    bases,
    incs,
    locals_,
    parts,
    state,
    kv_s,
    kv_r,
    q_s,
    q_r,
    o_s,
    o_r,
    z_s,
    z_r,
    e_s,
    e_r,
):
    at = Place()
    me = at.me
    kv_sem, q_sem, o_sem, z_sem, e_sem = (kv_s, kv_r), (q_s, q_r), (o_s, o_r), (z_s, z_r), (e_s, e_r)

    barrier = pltpu.get_barrier_semaphore()

    def greet(device):
        pl.semaphore_signal(barrier, inc=1, device_id=device, device_id_type=MESH)

    greet(at.target(0, 1)[2])
    loop(1, TILES, lambda t: [greet(at.target(t, core)[2]) for core in (0, 1)])
    loop(1, 8, lambda off: greet(at.along(off)[1]))

    flat_a[...] = k_ref[...].astype(F32).reshape(TOK * HEADS, HD)
    flat_b[...] = v_ref[...].astype(F32).reshape(TOK * HEADS, HD)
    rates[...] = rate_ref[...].astype(F32)
    row = lax.broadcasted_iota(jnp.int32, (META, TOK), 0)
    named = route_ref[...].astype(F32)
    high, low = split_rows(weight_ref[...])
    common = jnp.zeros((META, TOK), F32)
    lines = (named[0:1], named[1:2], high[0:1], low[0:1], high[1:2], low[1:2])
    for i, line in enumerate(lines):
        common = jnp.where(row == i + 1, line, common)

    pl.semaphore_wait(barrier, 38)

    def by_head(flat, d):
        return flat[pl.ds(d, TOK, stride=HEADS), :]

    def pack_kv(d, dest, slot):
        dest[slot, 0:TOK, :] = by_head(flat_a, d).astype(BF)
        dest[slot, TOK : TOK + META, :] = jnp.where(row == 0, rates[pl.ds(d, 1), :], common).astype(BF)
        dest[slot, TOK + META :, :] = by_head(flat_b, d).T.astype(BF)

    def kv_copy(chip, core):
        _, d, device = at.target(chip, core)
        return remote(slabs.at[d], got.at[me], kv_sem, 2 * chip + core, device)

    def send_kv(chip, core):
        d = at.target(chip, core)[1]
        pack_kv(d, slabs, d)
        kv_copy(chip, core).start()

    send_kv(0, 1)
    loop(1, TILES, lambda t: [send_kv(t, core) for core in (0, 1)])
    pack_kv(me, got, me)

    flat_a[...] = q_ref[...].astype(F32).reshape(TOK * HEADS, HD)

    def q_copy(chip, core):
        _, d, device = at.target(chip, core)
        return remote(q_out.at[d], q_got.at[me], q_sem, 2 * chip + core, device)

    def send_q(chip, core):
        d = at.target(chip, core)[1]
        q_out[d] = by_head(flat_a, d).T.astype(BF)
        q_copy(chip, core).start()

    send_q(0, 1)
    loop(1, TILES, lambda t: [send_q(t, core) for core in (0, 1)])
    q_got[me] = by_head(flat_a, me).T.astype(BF)

    first = lax.broadcasted_iota(jnp.int32, (PAIR, PAIR), 0)
    second = lax.broadcasted_iota(jnp.int32, (PAIR, PAIR), 1)
    causal = first <= second

    def gather_tile(c):
        meta = tile_meta(got, c)
        oh0, oh1 = tile_masks(meta)
        mask = oh0 + oh1
        upper = jnp.where(causal, 1.0, 0.0).astype(BF)
        run = dot((mask * meta[0:1, :]).astype(BF), upper)
        sums[pl.ds(c * MEM, MEM), :] = run
        kept = mask * jnp.exp(run[:, PAIR - 1 : PAIR] - run)
        wide = pair_values(got, c).astype(F32)
        scaled = jnp.concatenate(
            [(wide * kept[m : m + 1, :]).astype(BF) for m in range(MEM)], axis=0
        )
        incs[c] = dot(scaled, pair_keys(got, c))

    kv_copy(0, 1).wait_recv()
    gather_tile(at.source(0, 0)[0])

    def arrived(t):
        for core in (0, 1):
            kv_copy(t, core).wait_recv()
        gather_tile(at.source(t, 0)[0])

    loop(1, TILES, arrived)

    state[...] = jnp.zeros_like(state)

    def advance(c, base):
        locals_[c] = state[...].astype(BF)
        bases[pl.ds(c * MEM, MEM), :] = jnp.broadcast_to(base, (MEM, HD))
        total = sums[pl.ds(c * MEM, MEM), :][:, PAIR - 1 : PAIR]
        gone = jnp.exp(total)
        for m in range(MEM):
            cols = slice(m * HD, (m + 1) * HD)
            state[:, cols] = state[:, cols] * gone[m : m + 1, :] + incs[c, cols, :]
        return base + total

    whole = lax.fori_loop(0, TILES, advance, jnp.zeros((MEM, 1), F32))
    left_h, left_l = split_rows(jnp.exp(whole))
    for m in range(MEM):
        z_out[m, 0:HD, :] = state[:, m * HD : (m + 1) * HD].astype(BF)
        z_out[m, HD:, :] = jnp.where(row == 0, left_h[m : m + 1, :], left_l[m : m + 1, :]).astype(BF)

    def z_copy(off):
        to, device = at.along(off)
        return remote(z_out.at[to], z_got.at[at.z], z_sem, off, device)

    loop(1, 8, lambda off: z_copy(off).start())
    z_got[at.z] = z_out[at.z]

    def inside_tile(c):
        meta = tile_meta(got, c)
        oh0, oh1 = tile_masks(meta)
        run = sums[pl.ds(c * MEM, MEM), :]
        middle = 0.5 * run[:, PAIR - 1 : PAIR]
        up = jnp.exp(run - middle) * SCALE
        down_h, down_l = split_rows((oh0 + oh1) * jnp.exp(middle - run))
        below = jnp.concatenate([down_h, down_l, down_h, down_l], axis=0).astype(BF)
        vt = pair_values(got, c)
        qt = jnp.concatenate([q_got[2 * c], q_got[2 * c + 1]], axis=1)
        scores = dot(pair_keys(got, c), qt)
        reach = jnp.exp(run) * SCALE
        for j, oh in enumerate((oh0, oh1)):
            up_h, up_l = split_rows(oh * up)
            above = jnp.concatenate([up_h, up_h, up_l, up_l], axis=0).astype(BF)
            decay = lax.dot_general(
                below, above, (((0,), (0,)), ((), ())), preferred_element_type=F32
            )
            weights = jnp.where(causal, scores * decay, 0.0).astype(BF)
            across = dot(locals_[c], chosen_queries(qt, oh))
            parts[c, j] = dot(vt, weights) + across * jnp.sum(oh * reach, axis=0, keepdims=True)

    def inside(t):
        for core in (0, 1):
            q_copy(t, core).wait_recv()
        inside_tile(at.source(t, 0)[0])

    q_copy(0, 1).wait_recv()
    inside_tile(at.source(0, 0)[0])
    loop(1, TILES // 2, inside)

    loop(1, 8, lambda off: z_copy(off).wait_recv())
    entering = jnp.zeros((HD, HD), F32)
    for z in range(8):
        e_out[z] = entering.astype(BF)
        left = z_got[z, HD : HD + META, :].astype(F32)
        entering = entering * (left[0:1, :] + left[1:2, :]) + z_got[z, 0:HD, :].astype(F32)

    def e_copy(off):
        to, device = at.along(off)
        return remote(e_out.at[to], e_got.at[at.z], e_sem, off, device)

    loop(1, 8, lambda off: e_copy(off).start())
    e_got[at.z] = e_out[at.z]

    loop(TILES // 2, TILES, inside)

    loop(1, 8, lambda off: e_copy(off).wait_recv())
    for m in range(MEM):
        enter[:, m * HD : (m + 1) * HD] = e_got[m]
    gain = gain_ref[pl.ds(me, 1), :]

    def finish_tile(c):
        meta = tile_meta(got, c)
        qt = jnp.concatenate([q_got[2 * c], q_got[2 * c + 1]], axis=1)
        base = bases[pl.ds(c * MEM, MEM), :][:, 0:1]
        reach = jnp.exp(sums[pl.ds(c * MEM, MEM), :] + base) * SCALE
        mixed = jnp.zeros((HD, PAIR), F32)
        for j, oh in enumerate(tile_masks(meta)):
            across = dot(enter[...], chosen_queries(qt, oh))
            full = parts[c, j] + across * jnp.sum(oh * reach, axis=0, keepdims=True)
            square = jnp.mean(full * full, axis=0, keepdims=True)
            weight = meta[3 + 2 * j : 4 + 2 * j, :] + meta[4 + 2 * j : 5 + 2 * j, :]
            mixed = mixed + full * (lax.rsqrt(square + 1e-06) * weight)
        return (mixed.T * gain).astype(BF)

    def o_copy(chip, core):
        _, d, device = at.target(chip, core)
        return remote(o_out.at[d], o_got.at[me], o_sem, 2 * chip + core, device)

    def finish(t):
        c = at.target(t, 0)[0]
        done = finish_tile(c)
        o_out[2 * c] = done[0:TOK]
        o_out[2 * c + 1] = done[TOK:]
        for core in (0, 1):
            o_copy(t, core).start()

    loop(1, TILES, finish)
    home = at.target(0, 0)[0]
    done = finish_tile(home)
    o_out[2 * home] = done[0:TOK]
    o_out[2 * home + 1] = done[TOK:]
    o_copy(0, 1).start()
    o_got[me] = o_out[me]

    def unpack(s):
        out_ref[pl.ds(s, TOK, stride=HEADS), :] = o_got[s].astype(F32)

    def returned(t):
        for core in (0, 1):
            o_copy(t, core).wait_recv()
            unpack(at.source(t, core)[1])

    loop(1, TILES, returned)
    o_copy(0, 1).wait_recv()
    unpack(at.source(0, 1)[1])
    unpack(me)

    for copy in (kv_copy, q_copy, o_copy):
        copy(0, 1).wait_send()
        loop(1, TILES, lambda t, copy=copy: [copy(t, core).wait_send() for core in (0, 1)])
    for copy in (z_copy, e_copy):
        loop(1, 8, lambda off, copy=copy: copy(off).wait_send())


def shards(queries, keys, values, log_decay, routes, route_weight, gain):
    sems = [pltpu.SemaphoreType.DMA((HEADS,))] * 6 + [pltpu.SemaphoreType.DMA((8,))] * 4
    out = pl.pallas_call(
        layer_kernel,
        out_shape=jax.ShapeDtypeStruct((TOK * HEADS, HD), F32),
        in_specs=[pl.BlockSpec(memory_space=pltpu.VMEM)] * 7,
        out_specs=pl.BlockSpec(memory_space=pltpu.VMEM),
        scratch_shapes=[
            pltpu.VMEM((TOK * HEADS, HD), F32),
            pltpu.VMEM((TOK * HEADS, HD), F32),
            pltpu.VMEM((HEADS, TOK), F32),
            pltpu.VMEM((HEADS, SLAB, HD), BF),
            pltpu.VMEM((HEADS, SLAB, HD), BF),
            pltpu.VMEM((HEADS, HD, TOK), BF),
            pltpu.VMEM((HEADS, HD, TOK), BF),
            pltpu.VMEM((HEADS, TOK, HD), BF),
            pltpu.VMEM((HEADS, TOK, HD), BF),
            pltpu.VMEM((MEM, HD + META, HD), BF),
            pltpu.VMEM((MEM, HD + META, HD), BF),
            pltpu.VMEM((8, HD, HD), BF),
            pltpu.VMEM((8, HD, HD), BF),
            pltpu.VMEM((HD, MEM * HD), BF),
            pltpu.VMEM((TILES * MEM, PAIR), F32),
            pltpu.VMEM((TILES * MEM, HD), F32),
            pltpu.VMEM((TILES, MEM * HD, HD), F32),
            pltpu.VMEM((TILES, HD, MEM * HD), BF),
            pltpu.VMEM((TILES, 2, HD, PAIR), F32),
            pltpu.VMEM((HD, MEM * HD), F32),
            *sems,
        ],
        compiler_params=pltpu.CompilerParams(
            collective_id=0, has_side_effects=True, vmem_limit_bytes=50 * 1024 * 1024
        ),
        cost_estimate=pl.CostEstimate(
            flops=8 * 10**9, bytes_accessed=6 * 2**20, transcendentals=10**6
        ),
    )(
        queries[0],
        keys[0],
        values[0],
        log_decay[0].T,
        routes[0].T,
        route_weight[0].T,
        gain.reshape(HEADS, HD),
    )
    return out.astype(BF).reshape(1, TOK, HEADS, HD)


def solution(mesh):
    finer = Mesh(mesh.devices.reshape(4, 2, 8, 4), ("mem_0", "mem_1", "ctx_0", "ctx_1"))
    ctx = ("ctx_0", "ctx_1")
    mem = ("mem_0", "mem_1")
    return jax.shard_map(
        shards,
        mesh=finer,
        in_specs=(
            P(ctx, mem, None, None),
            P(ctx, mem, None, None),
            P(ctx, mem, None, None),
            P(ctx, mem, None),
            P(ctx, mem, None),
            P(ctx, mem, None),
            P(),
        ),
        out_specs=P(ctx, mem, None, None),
        check_vma=False,
    )
```

time: 179 us -> 103 us (0.58)
  blocking collectives: 90.6 us -> 0 us
  Pallas kernels: 47.6 us -> 93.3 us
  waiting for transfers between devices: 26.7 us -> 0 us
  starting transfers between devices: 8.43 us -> 0 us
  local copies, waits for them, and re-layouts: 2.31 us -> 6.44 us
    all_to_all x4 -> x0, blocking collectives: 90.6 us -> none  [exchange(): return lax.all_to_all(parts, axes, split_axis=0, concat_axis=0, tiled=True)]
    pallas_call x5 -> x1, Pallas kernels: 47.6 us -> 93.3 us  [shards(): pl.pallas_call(layer_kernel, out_shape=jax.ShapeDtypeStruct((TOK * HEADS,...]
    all_to_all x2 -> x0, waiting for transfers between devices: 26.7 us -> none  [exchange(): return lax.all_to_all(parts, axes, split_axis=0, concat_axis=0, tiled=True)]
    all_to_all x2 -> x0, starting transfers between devices: 8.43 us -> none  [exchange(): return lax.all_to_all(parts, axes, split_axis=0, concat_axis=0, tiled=True)]
    unnamed x8 -> x14, local copies, waits for them, and re-layouts: 0.72 us -> 6.44 us
  transfers between devices with their start and end apart: 2 -> 0, of which waited for: 2 -> 0; matrix products, arithmetic and copies ran while one was open for 0% -> 0% of each run, Pallas kernels for 1% -> 0%
where the time goes in v2:
time: 103 us; the launch traced here: 102 us
  Pallas kernels  93.3 us (91%)
  local copies, waits for them, and re-layouts  6.44 us (6%)
  other arithmetic  2.66 us (3%)
    pallas_call x1, Pallas kernels, shards(): pl.pallas_call(layer_kernel, out_shape=jax.ShapeDtypeStruct((TOK * HEADS,...  93.3 us
    unnamed x14, local copies, waits for them, and re-layouts  6.44 us
    convert_element_type x1, other arithmetic, shards(): return out.astype(BF).reshape(1, TOK, HEADS, HD)  2.66 us

profile of v2, /device:TPU:1, one launch (start us, length us, event | category | flops | bytes accessed | tf_op | source)
XLA Modules:
  0.0 102.4 jit_solution(15007683385924854681)
XLA Ops:
  0.0 0.0 copy-start
  0.0 1.2 %copy-done = bf16[1,128,32,128]{3,2,1,0:T(8,128)(2,1)S(1)} copy-done((bf16[1,128,32,128]{3,2,1,0:T(8,128)(2,1)S(1)}, bf16[1,128,32,128]{3,2,1,0:T(8,128)(2,1)}, u32[]{:S(2)}) %copy-start) | copy-done | bytes 1048600
  1.2 0.0 copy-start.1
  1.2 1.2 %copy-done.1 = bf16[1,128,32,128]{3,2,1,0:T(8,128)(2,1)S(1)} copy-done((bf16[1,128,32,128]{3,2,1,0:T(8,128)(2,1)S(1)}, bf16[1,128,32,128]{3,2,1,0:T(8,128)(2,1)}, u32[]{:S(2)}) %copy-start.1) | copy-done | bytes 1048600
  2.5 0.0 copy-start.2
  2.5 1.2 %copy-done.2 = bf16[1,128,32,128]{3,2,1,0:T(8,128)(2,1)S(1)} copy-done((bf16[1,128,32,128]{3,2,1,0:T(8,128)(2,1)S(1)}, bf16[1,128,32,128]{3,2,1,0:T(8,128)(2,1)}, u32[]{:S(2)}) %copy-start.2) | copy-done | bytes 1048600
  3.7 0.0 copy-start.3
  3.7 0.7 copy-done.3
  4.4 0.0 copy-start.4
  4.4 0.7 copy-done.4
  5.1 0.0 copy-start.5
  5.1 0.7 copy-done.5
  5.8 0.0 copy-start.6
  5.8 0.7 copy-done.6
  6.5 93.3 %shard_map.73 = f32[4096,128]{1,0:T(8,128)} custom-call(bf16[128,32,128]{2,1,0:T(8,128)(2,1)S(1)} %bitcast.14, bf16[128,32,128]{2,1,0:T(8,128)(2,1)S(1)} %bitcast.15, bf16[128,32,128]{2,1,0:T(8,128)(2,1)S(1)} %bitcast.16, bf16[32,128]{1,0:T(8,128)(2,1)S(1)} %bitcast.18, s32[2,128]{1,0:T(2,128)S(1)} %bitcast.19, f32[2,128]{1,0:T(2,128)S(1)} %bitcast.20, ...), custom_call_target="tpu_custom_call" | custom-call | flops 8000000000 | bytes 6291456 | tf_op jit(solution)/shard_map/pallas_call | solution.py:367
  99.7 2.7 %convert_element_type.3 = bf16[4096,128]{1,0:T(8,128)(2,1)} convert(f32[4096,128]{1,0:T(8,128)} %shard_map.73) | non-fusion elementwise | flops 524288 | bytes 3145728 | tf_op jit(solution)/shard_map/convert_element_type | solution.py:410
Async XLA Ops:
  0.0 1.2 %copy-start = (bf16[1,128,32,128]{3,2,1,0:T(8,128)(2,1)S(1)}, bf16[1,128,32,128]{3,2,1,0:T(8,128)(2,1)}, u32[]{:S(2)}) copy-start(bf16[1,128,32,128]{3,2,1,0:T(8,128)(2,1)} %param.7) | copy-start | bytes 3145732
  1.2 1.2 %copy-start.1 = (bf16[1,128,32,128]{3,2,1,0:T(8,128)(2,1)S(1)}, bf16[1,128,32,128]{3,2,1,0:T(8,128)(2,1)}, u32[]{:S(2)}) copy-start(bf16[1,128,32,128]{3,2,1,0:T(8,128)(2,1)} %param.8) | copy-start | bytes 3145732
  2.5 1.2 %copy-start.2 = (bf16[1,128,32,128]{3,2,1,0:T(8,128)(2,1)S(1)}, bf16[1,128,32,128]{3,2,1,0:T(8,128)(2,1)}, u32[]{:S(2)}) copy-start(bf16[1,128,32,128]{3,2,1,0:T(8,128)(2,1)} %param.9) | copy-start | bytes 3145732
  3.7 0.7 copy-start.3
  4.4 0.7 copy-start.4
  5.1 0.7 copy-start.5
  5.8 0.7 copy-start.6

commit v3 on v2

--- a/solution.py
+++ b/solution.py
@@ -13,6 +13,8 @@
 META = 16
 PAIR = 2 * TOK
 TILES = HEADS // 2
+EARLY = 6
+FIRST = 6
 SLAB = TOK + META + HD
 BF = jnp.bfloat16
 F32 = jnp.float32
@@ -24,6 +26,27 @@
     return jnp.dot(a, b, preferred_element_type=F32)
 
 
+ORDER = (
+    ((0, 0), (1, 3), (3, 1), (2, 2), (1, 1), (3, 3), (1, 2), (3, 2))
+    + ((2, 1), (2, 3), (0, 1), (1, 0), (0, 3), (3, 0), (0, 2), (2, 0))
+)
+
+
+def coded(values):
+    whole = sum(v << (2 * i) for i, v in enumerate(values))
+    return whole - (1 << 32) if whole >= 1 << 31 else whole
+
+
+STEP_X, STEP_Y = coded([a for a, _ in ORDER]), coded([b for _, b in ORDER])
+
+
+def offset(chip):
+    if isinstance(chip, int):
+        return ORDER[chip]
+    turn = 2 * chip
+    return tuple(jnp.bitwise_and(jnp.right_shift(jnp.int32(w), turn), 3) for w in (STEP_X, STEP_Y))
+
+
 class Place:
     def __init__(self):
         self.x, self.y = lax.axis_index("ctx_1"), lax.axis_index("mem_0")
@@ -31,14 +54,13 @@
         self.me = (self.x * 4 + self.y) * 2 + self.c
 
     def target(self, chip, core):
-        x, y = lax.rem(self.x + chip // 4, 4), lax.rem(self.y + lax.rem(chip, 4), 4)
-        c = lax.rem(self.c + core, 2)
+        dx, dy = offset(chip)
+        x, y, c = lax.rem(self.x + dx, 4), lax.rem(self.y + dy, 4), lax.rem(self.c + core, 2)
         return x * 4 + y, (x * 4 + y) * 2 + c, {"ctx_1": x, "mem_0": y, "mem_1": c}
 
     def source(self, chip, core):
-        x = lax.rem(self.x + 4 - chip // 4, 4)
-        y = lax.rem(self.y + 4 - lax.rem(chip, 4), 4)
-        c = lax.rem(self.c + core, 2)
+        dx, dy = offset(chip)
+        x, y, c = lax.rem(self.x + 4 - dx, 4), lax.rem(self.y + 4 - dy, 4), lax.rem(self.c + core, 2)
         return x * 4 + y, (x * 4 + y) * 2 + c
 
     def along(self, off):
@@ -92,6 +114,10 @@
     return high, rows - high
 
 
+def side_by_side(states):
+    return jnp.concatenate([states[m] for m in range(MEM)], axis=1)
+
+
 def chosen_queries(qt, oh):
     grouped = qt.reshape(HD // 16, 16, PAIR)
     parts = []
@@ -110,6 +136,13 @@
     weight_ref,
     gain_ref,
     out_ref,
+    q_here,
+    k_here,
+    v_here,
+    rate_here,
+    route_here,
+    weight_here,
+    gain_here,
     flat_a,
     flat_b,
     rates,
@@ -123,13 +156,13 @@
     z_got,
     e_out,
     e_got,
-    enter,
+    left,
+    totals,
     sums,
     bases,
     incs,
     locals_,
     parts,
-    state,
     kv_s,
     kv_r,
     q_s,
@@ -140,11 +173,28 @@
     z_r,
     e_s,
     e_r,
+    in_s,
 ):
     at = Place()
     me = at.me
     kv_sem, q_sem, o_sem, z_sem, e_sem = (kv_s, kv_r), (q_s, q_r), (o_s, o_r), (z_s, z_r), (e_s, e_r)
 
+    fetches = [
+        pltpu.make_async_copy(there, here, in_s.at[i])
+        for i, (there, here) in enumerate(
+            (
+                (k_ref, k_here),
+                (v_ref, v_here),
+                (rate_ref, rate_here),
+                (route_ref, route_here),
+                (weight_ref, weight_here),
+                (gain_ref, gain_here),
+                (q_ref, q_here),
+            )
+        )
+    ]
+    for fetch in fetches:
+        fetch.start()
     barrier = pltpu.get_barrier_semaphore()
 
     def greet(device):
@@ -154,19 +204,21 @@
     loop(1, TILES, lambda t: [greet(at.target(t, core)[2]) for core in (0, 1)])
     loop(1, 8, lambda off: greet(at.along(off)[1]))
 
-    flat_a[...] = k_ref[...].astype(F32).reshape(TOK * HEADS, HD)
-    flat_b[...] = v_ref[...].astype(F32).reshape(TOK * HEADS, HD)
-    rates[...] = rate_ref[...].astype(F32)
+    fetches[0].wait()
+    flat_a[...] = k_here[...].astype(F32).reshape(TOK * HEADS, HD)
+    fetches[1].wait()
+    flat_b[...] = v_here[...].astype(F32).reshape(TOK * HEADS, HD)
+    for fetch in fetches[2:]:
+        fetch.wait()
+    rates[...] = rate_here[...].astype(F32)
     row = lax.broadcasted_iota(jnp.int32, (META, TOK), 0)
-    named = route_ref[...].astype(F32)
-    high, low = split_rows(weight_ref[...])
+    named = route_here[...].astype(F32)
+    high, low = split_rows(weight_here[...])
     common = jnp.zeros((META, TOK), F32)
     lines = (named[0:1], named[1:2], high[0:1], low[0:1], high[1:2], low[1:2])
     for i, line in enumerate(lines):
         common = jnp.where(row == i + 1, line, common)
 
-    pl.semaphore_wait(barrier, 38)
-
     def by_head(flat, d):
         return flat[pl.ds(d, TOK, stride=HEADS), :]
 
@@ -179,28 +231,40 @@
         _, d, device = at.target(chip, core)
         return remote(slabs.at[d], got.at[me], kv_sem, 2 * chip + core, device)
 
-    def send_kv(chip, core):
-        d = at.target(chip, core)[1]
-        pack_kv(d, slabs, d)
-        kv_copy(chip, core).start()
-
-    send_kv(0, 1)
-    loop(1, TILES, lambda t: [send_kv(t, core) for core in (0, 1)])
+    def pack_pair(t):
+        for core in (0, 1):
+            d = at.target(t, core)[1]
+            pack_kv(d, slabs, d)
+
+    def start_pair(copy, t):
+        for core in (0, 1):
+            copy(t, core).start()
+
+    loop(1, EARLY, pack_pair)
+    pl.semaphore_wait(barrier, 38)
+    loop(1, EARLY, lambda t: start_pair(kv_copy, t))
+
+    def pack_and_start(t):
+        pack_pair(t)
+        start_pair(kv_copy, t)
+
+    loop(EARLY, TILES, pack_and_start)
+    sibling = at.target(0, 1)[1]
+    pack_kv(sibling, slabs, sibling)
+    kv_copy(0, 1).start()
     pack_kv(me, got, me)
 
-    flat_a[...] = q_ref[...].astype(F32).reshape(TOK * HEADS, HD)
+    flat_a[...] = q_here[...].astype(F32).reshape(TOK * HEADS, HD)
 
     def q_copy(chip, core):
         _, d, device = at.target(chip, core)
         return remote(q_out.at[d], q_got.at[me], q_sem, 2 * chip + core, device)
 
-    def send_q(chip, core):
-        d = at.target(chip, core)[1]
-        q_out[d] = by_head(flat_a, d).T.astype(BF)
-        q_copy(chip, core).start()
-
-    send_q(0, 1)
-    loop(1, TILES, lambda t: [send_q(t, core) for core in (0, 1)])
+    def pack_q(d, dest):
+        dest[d] = by_head(flat_a, d).T.astype(BF)
+
+    loop(1, TILES, lambda t: [pack_q(at.target(t, core)[1], q_out) for core in (0, 1)])
+    pack_q(sibling, q_out)
     q_got[me] = by_head(flat_a, me).T.astype(BF)
 
     first = lax.broadcasted_iota(jnp.int32, (PAIR, PAIR), 0)
@@ -214,12 +278,14 @@
         upper = jnp.where(causal, 1.0, 0.0).astype(BF)
         run = dot((mask * meta[0:1, :]).astype(BF), upper)
         sums[pl.ds(c * MEM, MEM), :] = run
-        kept = mask * jnp.exp(run[:, PAIR - 1 : PAIR] - run)
+        total = run[:, PAIR - 1 : PAIR]
+        totals[pl.ds(c * MEM, MEM), :] = jnp.broadcast_to(total, (MEM, HD))
+        kept = mask * jnp.exp(total - run)
         wide = pair_values(got, c).astype(F32)
         scaled = jnp.concatenate(
             [(wide * kept[m : m + 1, :]).astype(BF) for m in range(MEM)], axis=0
         )
-        incs[c] = dot(scaled, pair_keys(got, c))
+        incs[c] = dot(scaled, pair_keys(got, c)).reshape(MEM, HD, HD)
 
     kv_copy(0, 1).wait_recv()
     gather_tile(at.source(0, 0)[0])
@@ -231,29 +297,45 @@
 
     loop(1, TILES, arrived)
 
-    state[...] = jnp.zeros_like(state)
-
-    def advance(c, base):
-        locals_[c] = state[...].astype(BF)
-        bases[pl.ds(c * MEM, MEM), :] = jnp.broadcast_to(base, (MEM, HD))
-        total = sums[pl.ds(c * MEM, MEM), :][:, PAIR - 1 : PAIR]
-        gone = jnp.exp(total)
-        for m in range(MEM):
-            cols = slice(m * HD, (m + 1) * HD)
-            state[:, cols] = state[:, cols] * gone[m : m + 1, :] + incs[c, cols, :]
+    def add_total(c, base):
+        at_c = pl.ds(c * MEM, MEM)
+        total = totals[at_c, :]
+        bases[at_c, :] = base
+        totals[at_c, :] = jnp.exp(total)
         return base + total
 
-    whole = lax.fori_loop(0, TILES, advance, jnp.zeros((MEM, 1), F32))
+    whole = lax.fori_loop(0, TILES, add_total, jnp.zeros((MEM, HD), F32))
     left_h, left_l = split_rows(jnp.exp(whole))
-    for m in range(MEM):
-        z_out[m, 0:HD, :] = state[:, m * HD : (m + 1) * HD].astype(BF)
-        z_out[m, HD:, :] = jnp.where(row == 0, left_h[m : m + 1, :], left_l[m : m + 1, :]).astype(BF)
+    left[0:MEM, :] = left_h
+    left[MEM:, :] = left_l
 
     def z_copy(off):
         to, device = at.along(off)
         return remote(z_out.at[to], z_got.at[at.z], z_sem, off, device)
 
-    loop(1, 8, lambda off: z_copy(off).start())
+    def memory_states(m):
+        def four(i, run):
+            for k in range(4):
+                c = 4 * i + k
+                locals_[c, m] = run.astype(BF)
+                run = run * totals[pl.ds(c * MEM + m, 1), :] + incs[c, m]
+            return run
+
+        run = lax.fori_loop(0, TILES // 4, four, jnp.zeros((HD, HD), F32))
+        z_out[m, 0:HD, :] = run.astype(BF)
+        lines = left[pl.ds(m, 1), :], left[pl.ds(MEM + m, 1), :]
+        z_out[m, HD:, :] = jnp.where(row == 0, *lines).astype(BF)
+
+    def send_states(off):
+        memory_states(at.along(off)[0])
+        z_copy(off).start()
+        start_pair(q_copy, 2 * off - 1)
+        start_pair(q_copy, 2 * off)
+
+    loop(1, 8, send_states)
+    start_pair(q_copy, TILES - 1)
+    q_copy(0, 1).start()
+    memory_states(at.z)
     z_got[at.z] = z_out[at.z]
 
     def inside_tile(c):
@@ -275,7 +357,7 @@
                 below, above, (((0,), (0,)), ((), ())), preferred_element_type=F32
             )
             weights = jnp.where(causal, scores * decay, 0.0).astype(BF)
-            across = dot(locals_[c], chosen_queries(qt, oh))
+            across = dot(side_by_side(locals_.at[c]), chosen_queries(qt, oh))
             parts[c, j] = dot(vt, weights) + across * jnp.sum(oh * reach, axis=0, keepdims=True)
 
     def inside(t):
@@ -285,7 +367,7 @@
 
     q_copy(0, 1).wait_recv()
     inside_tile(at.source(0, 0)[0])
-    loop(1, TILES // 2, inside)
+    loop(1, FIRST, inside)
 
     loop(1, 8, lambda off: z_copy(off).wait_recv())
     entering = jnp.zeros((HD, HD), F32)
@@ -301,12 +383,10 @@
     loop(1, 8, lambda off: e_copy(off).start())
     e_got[at.z] = e_out[at.z]
 
-    loop(TILES // 2, TILES, inside)
+    loop(FIRST, TILES, inside)
 
     loop(1, 8, lambda off: e_copy(off).wait_recv())
-    for m in range(MEM):
-        enter[:, m * HD : (m + 1) * HD] = e_got[m]
-    gain = gain_ref[pl.ds(me, 1), :]
+    gain = gain_here[pl.ds(me, 1), :]
 
     def finish_tile(c):
         meta = tile_meta(got, c)
@@ -315,7 +395,7 @@
         reach = jnp.exp(sums[pl.ds(c * MEM, MEM), :] + base) * SCALE
         mixed = jnp.zeros((HD, PAIR), F32)
         for j, oh in enumerate(tile_masks(meta)):
-            across = dot(enter[...], chosen_queries(qt, oh))
+            across = dot(side_by_side(e_got), chosen_queries(qt, oh))
             full = parts[c, j] + across * jnp.sum(oh * reach, axis=0, keepdims=True)
             square = jnp.mean(full * full, axis=0, keepdims=True)
             weight = meta[3 + 2 * j : 4 + 2 * j, :] + meta[4 + 2 * j : 5 + 2 * j, :]
@@ -367,9 +447,16 @@
     out = pl.pallas_call(
         layer_kernel,
         out_shape=jax.ShapeDtypeStruct((TOK * HEADS, HD), F32),
-        in_specs=[pl.BlockSpec(memory_space=pltpu.VMEM)] * 7,
+        in_specs=[pl.BlockSpec(memory_space=pltpu.HBM)] * 7,
         out_specs=pl.BlockSpec(memory_space=pltpu.VMEM),
         scratch_shapes=[
+            pltpu.VMEM((TOK, HEADS, HD), BF),
+            pltpu.VMEM((TOK, HEADS, HD), BF),
+            pltpu.VMEM((TOK, HEADS, HD), BF),
+            pltpu.VMEM((HEADS, TOK), BF),
+            pltpu.VMEM((2, TOK), jnp.int32),
+            pltpu.VMEM((2, TOK), F32),
+            pltpu.VMEM((HEADS, HD), F32),
             pltpu.VMEM((TOK * HEADS, HD), F32),
             pltpu.VMEM((TOK * HEADS, HD), F32),
             pltpu.VMEM((HEADS, TOK), F32),
@@ -383,17 +470,18 @@
             pltpu.VMEM((MEM, HD + META, HD), BF),
             pltpu.VMEM((8, HD, HD), BF),
             pltpu.VMEM((8, HD, HD), BF),
-            pltpu.VMEM((HD, MEM * HD), BF),
+            pltpu.VMEM((2 * MEM, HD), F32),
+            pltpu.VMEM((TILES * MEM, HD), F32),
             pltpu.VMEM((TILES * MEM, PAIR), F32),
             pltpu.VMEM((TILES * MEM, HD), F32),
-            pltpu.VMEM((TILES, MEM * HD, HD), F32),
-            pltpu.VMEM((TILES, HD, MEM * HD), BF),
+            pltpu.VMEM((TILES, MEM, HD, HD), F32),
+            pltpu.VMEM((TILES, MEM, HD, HD), BF),
             pltpu.VMEM((TILES, 2, HD, PAIR), F32),
-            pltpu.VMEM((HD, MEM * HD), F32),
             *sems,
+            pltpu.SemaphoreType.DMA((7,)),
         ],
         compiler_params=pltpu.CompilerParams(
-            collective_id=0, has_side_effects=True, vmem_limit_bytes=50 * 1024 * 1024
+            collective_id=0, has_side_effects=True, vmem_limit_bytes=60 * 1024 * 1024
         ),
         cost_estimate=pl.CostEstimate(
             flops=8 * 10**9, bytes_accessed=6 * 2**20, transcendentals=10**6

time: 103 us -> 84.2 us (0.82)
  Pallas kernels: 93.3 us -> 81.4 us
  local copies, waits for them, and re-layouts: 6.44 us -> 0 us
    pallas_call x1, Pallas kernels: 93.3 us -> 81.4 us  [shards(): pl.pallas_call(layer_kernel, out_shape=jax.ShapeDtypeStruct((TOK * HEADS,...]
    unnamed x14 -> x0, local copies, waits for them, and re-layouts: 6.44 us -> none
where the time goes in v3:
time: 84.2 us; the launch traced here: 84.1 us
  Pallas kernels  81.4 us (97%)
  other arithmetic  2.66 us (3%)
    pallas_call x1, Pallas kernels, shards(): pl.pallas_call(layer_kernel, out_shape=jax.ShapeDtypeStruct((TOK * HEADS,...  81.4 us
    convert_element_type x1, other arithmetic, shards(): return out.astype(BF).reshape(1, TOK, HEADS, HD)  2.66 us

profile of v3, /device:TPU:1, one launch (start us, length us, event | category | flops | bytes accessed | tf_op | source)
XLA Modules:
  0.0 84.1 jit_solution(6553162519762359882)
XLA Ops:
  0.0 81.4 %shard_map.73 = f32[4096,128]{1,0:T(8,128)} custom-call(bf16[128,32,128]{2,1,0:T(8,128)(2,1)} %bitcast.14, bf16[128,32,128]{2,1,0:T(8,128)(2,1)} %bitcast.15, bf16[128,32,128]{2,1,0:T(8,128)(2,1)} %bitcast.16, bf16[32,128]{1,0:T(8,128)(2,1)} %bitcast.18, s32[2,128]{1,0:T(2,128)} %bitcast.19, f32[2,128]{1,0:T(2,128)} %bitcast.20, f32[32,128]{1,0:T(8,128)} %bitcast.17), custom_call_target="tpu_custom_call" | custom-call | flops 8000000000 | bytes 6291456 | tf_op jit(solution)/shard_map/pallas_call | solution.py:447
  81.4 2.7 %convert_element_type.3 = bf16[4096,128]{1,0:T(8,128)(2,1)} convert(f32[4096,128]{1,0:T(8,128)} %shard_map.73) | non-fusion elementwise | flops 524288 | bytes 3145728 | tf_op jit(solution)/shard_map/convert_element_type | solution.py:498

commit v4 on v3

--- a/solution.py
+++ b/solution.py
@@ -14,7 +14,7 @@
 PAIR = 2 * TOK
 TILES = HEADS // 2
 EARLY = 6
-FIRST = 6
+FIRST = 1
 SLAB = TOK + META + HD
 BF = jnp.bfloat16
 F32 = jnp.float32
@@ -151,7 +151,6 @@
     q_out,
     q_got,
     o_out,
-    o_got,
     z_out,
     z_got,
     e_out,
@@ -204,10 +203,17 @@
     loop(1, TILES, lambda t: [greet(at.target(t, core)[2]) for core in (0, 1)])
     loop(1, 8, lambda off: greet(at.along(off)[1]))
 
+    def widen(flat, here):
+        def some(i):
+            rows = here[pl.ds(i * 16, 16), :, :].astype(F32)
+            flat[pl.ds(i * 16 * HEADS, 16 * HEADS), :] = rows.reshape(16 * HEADS, HD)
+
+        loop(0, TOK // 16, some)
+
     fetches[0].wait()
-    flat_a[...] = k_here[...].astype(F32).reshape(TOK * HEADS, HD)
+    widen(flat_a, k_here)
     fetches[1].wait()
-    flat_b[...] = v_here[...].astype(F32).reshape(TOK * HEADS, HD)
+    widen(flat_b, v_here)
     for fetch in fetches[2:]:
         fetch.wait()
     rates[...] = rate_here[...].astype(F32)
@@ -236,25 +242,31 @@
             d = at.target(t, core)[1]
             pack_kv(d, slabs, d)
 
+    def others(t, act):
+        @pl.when(t > 0)
+        def _():
+            act(t, 0)
+
+        act(t, 1)
+
     def start_pair(copy, t):
-        for core in (0, 1):
-            copy(t, core).start()
-
-    loop(1, EARLY, pack_pair)
+        others(t, lambda chip, core: copy(chip, core).start())
+
+    def last_is_home(i):
+        return lax.rem(i + 1, TILES)
+
+    loop(0, EARLY, lambda i: pack_pair(i + 1))
     pl.semaphore_wait(barrier, 38)
-    loop(1, EARLY, lambda t: start_pair(kv_copy, t))
-
-    def pack_and_start(t):
-        pack_pair(t)
-        start_pair(kv_copy, t)
+    loop(0, EARLY, lambda i: start_pair(kv_copy, i + 1))
+
+    def pack_and_start(i):
+        pack_pair(last_is_home(i))
+        start_pair(kv_copy, last_is_home(i))
 
     loop(EARLY, TILES, pack_and_start)
-    sibling = at.target(0, 1)[1]
-    pack_kv(sibling, slabs, sibling)
-    kv_copy(0, 1).start()
-    pack_kv(me, got, me)
-
-    flat_a[...] = q_here[...].astype(F32).reshape(TOK * HEADS, HD)
+    got[me] = slabs[me]
+
+    widen(flat_a, q_here)
 
     def q_copy(chip, core):
         _, d, device = at.target(chip, core)
@@ -263,9 +275,8 @@
     def pack_q(d, dest):
         dest[d] = by_head(flat_a, d).T.astype(BF)
 
-    loop(1, TILES, lambda t: [pack_q(at.target(t, core)[1], q_out) for core in (0, 1)])
-    pack_q(sibling, q_out)
-    q_got[me] = by_head(flat_a, me).T.astype(BF)
+    loop(0, TILES, lambda t: [pack_q(at.target(t, core)[1], q_out) for core in (0, 1)])
+    q_got[me] = q_out[me]
 
     first = lax.broadcasted_iota(jnp.int32, (PAIR, PAIR), 0)
     second = lax.broadcasted_iota(jnp.int32, (PAIR, PAIR), 1)
@@ -287,15 +298,11 @@
         )
         incs[c] = dot(scaled, pair_keys(got, c)).reshape(MEM, HD, HD)
 
-    kv_copy(0, 1).wait_recv()
-    gather_tile(at.source(0, 0)[0])
-
     def arrived(t):
-        for core in (0, 1):
-            kv_copy(t, core).wait_recv()
+        others(t, lambda chip, core: kv_copy(chip, core).wait_recv())
         gather_tile(at.source(t, 0)[0])
 
-    loop(1, TILES, arrived)
+    loop(0, TILES, arrived)
 
     def add_total(c, base):
         at_c = pl.ds(c * MEM, MEM)
@@ -332,9 +339,9 @@
         start_pair(q_copy, 2 * off - 1)
         start_pair(q_copy, 2 * off)
 
+    q_copy(0, 1).start()
     loop(1, 8, send_states)
     start_pair(q_copy, TILES - 1)
-    q_copy(0, 1).start()
     memory_states(at.z)
     z_got[at.z] = z_out[at.z]
 
@@ -360,30 +367,30 @@
             across = dot(side_by_side(locals_.at[c]), chosen_queries(qt, oh))
             parts[c, j] = dot(vt, weights) + across * jnp.sum(oh * reach, axis=0, keepdims=True)
 
-    def inside(t):
-        for core in (0, 1):
-            q_copy(t, core).wait_recv()
-        inside_tile(at.source(t, 0)[0])
-
-    q_copy(0, 1).wait_recv()
-    inside_tile(at.source(0, 0)[0])
-    loop(1, FIRST, inside)
-
-    loop(1, 8, lambda off: z_copy(off).wait_recv())
-    entering = jnp.zeros((HD, HD), F32)
-    for z in range(8):
-        e_out[z] = entering.astype(BF)
-        left = z_got[z, HD : HD + META, :].astype(F32)
-        entering = entering * (left[0:1, :] + left[1:2, :]) + z_got[z, 0:HD, :].astype(F32)
-
     def e_copy(off):
         to, device = at.along(off)
         return remote(e_out.at[to], e_got.at[at.z], e_sem, off, device)
 
-    loop(1, 8, lambda off: e_copy(off).start())
-    e_got[at.z] = e_out[at.z]
-
-    loop(FIRST, TILES, inside)
+    def compose():
+        loop(1, 8, lambda off: z_copy(off).wait_recv())
+        entering = jnp.zeros((HD, HD), F32)
+        for z in range(8):
+            e_out[z] = entering.astype(BF)
+            kept = z_got[z, HD : HD + META, :].astype(F32)
+            entering = entering * (kept[0:1, :] + kept[1:2, :]) + z_got[z, 0:HD, :].astype(F32)
+        loop(1, 8, lambda off: e_copy(off).start())
+        e_got[at.z] = e_out[at.z]
+
+    def inside(t):
+        pl.when(t == FIRST)(compose)
+        others(t, lambda chip, core: q_copy(chip, core).wait_recv())
+        inside_tile(at.source(t, 0)[0])
+
+    loop(0, TILES, inside)
+    for copy in (kv_copy, q_copy):
+        sent = lambda chip, core, copy=copy: copy(chip, core).wait_send()
+        loop(0, TILES, lambda t, sent=sent: others(t, sent))
+    loop(1, 8, lambda off: z_copy(off).wait_send())
 
     loop(1, 8, lambda off: e_copy(off).wait_recv())
     gain = gain_here[pl.ds(me, 1), :]
@@ -404,51 +411,34 @@
 
     def o_copy(chip, core):
         _, d, device = at.target(chip, core)
-        return remote(o_out.at[d], o_got.at[me], o_sem, 2 * chip + core, device)
-
-    def finish(t):
+        return remote(o_out.at[d], out_ref.at[me], o_sem, 0, device)
+
+    def finish(i):
+        t = last_is_home(i)
         c = at.target(t, 0)[0]
         done = finish_tile(c)
         o_out[2 * c] = done[0:TOK]
         o_out[2 * c + 1] = done[TOK:]
-        for core in (0, 1):
-            o_copy(t, core).start()
-
-    loop(1, TILES, finish)
-    home = at.target(0, 0)[0]
-    done = finish_tile(home)
-    o_out[2 * home] = done[0:TOK]
-    o_out[2 * home + 1] = done[TOK:]
-    o_copy(0, 1).start()
-    o_got[me] = o_out[me]
-
-    def unpack(s):
-        out_ref[pl.ds(s, TOK, stride=HEADS), :] = o_got[s].astype(F32)
-
-    def returned(t):
-        for core in (0, 1):
-            o_copy(t, core).wait_recv()
-            unpack(at.source(t, core)[1])
-
-    loop(1, TILES, returned)
-    o_copy(0, 1).wait_recv()
-    unpack(at.source(0, 1)[1])
-    unpack(me)
-
-    for copy in (kv_copy, q_copy, o_copy):
-        copy(0, 1).wait_send()
-        loop(1, TILES, lambda t, copy=copy: [copy(t, core).wait_send() for core in (0, 1)])
-    for copy in (z_copy, e_copy):
-        loop(1, 8, lambda off, copy=copy: copy(off).wait_send())
+        start_pair(o_copy, t)
+
+    loop(0, TILES, finish)
+    own = pltpu.make_async_copy(o_out.at[me], out_ref.at[me], in_s.at[0])
+    own.start()
+    loop(1, 8, lambda off: e_copy(off).wait_send())
+    own.wait()
+    every = pl.ds(0, HEADS - 1)
+    whole_out = remote(o_out.at[every], out_ref.at[every], o_sem, 0, at.target(0, 1)[2])
+    whole_out.wait_recv()
+    whole_out.wait_send()
 
 
 def shards(queries, keys, values, log_decay, routes, route_weight, gain):
-    sems = [pltpu.SemaphoreType.DMA((HEADS,))] * 6 + [pltpu.SemaphoreType.DMA((8,))] * 4
+    sems = [pltpu.SemaphoreType.DMA((HEADS,))] * 4 + [pltpu.SemaphoreType.DMA((1,))] * 2 + [pltpu.SemaphoreType.DMA((8,))] * 4
     out = pl.pallas_call(
         layer_kernel,
-        out_shape=jax.ShapeDtypeStruct((TOK * HEADS, HD), F32),
+        out_shape=jax.ShapeDtypeStruct((HEADS, TOK, HD), BF),
         in_specs=[pl.BlockSpec(memory_space=pltpu.HBM)] * 7,
-        out_specs=pl.BlockSpec(memory_space=pltpu.VMEM),
+        out_specs=pl.BlockSpec(memory_space=pltpu.HBM),
         scratch_shapes=[
             pltpu.VMEM((TOK, HEADS, HD), BF),
             pltpu.VMEM((TOK, HEADS, HD), BF),
@@ -464,7 +454,6 @@
             pltpu.VMEM((HEADS, SLAB, HD), BF),
             pltpu.VMEM((HEADS, HD, TOK), BF),
             pltpu.VMEM((HEADS, HD, TOK), BF),
-            pltpu.VMEM((HEADS, TOK, HD), BF),
             pltpu.VMEM((HEADS, TOK, HD), BF),
             pltpu.VMEM((MEM, HD + META, HD), BF),
             pltpu.VMEM((MEM, HD + META, HD), BF),
@@ -495,7 +484,7 @@
         route_weight[0].T,
         gain.reshape(HEADS, HD),
     )
-    return out.astype(BF).reshape(1, TOK, HEADS, HD)
+    return jnp.swapaxes(out, 0, 1)[None]
 
 
 def solution(mesh):

time: 84.2 us -> 82.5 us (0.980)
  local copies, waits for them, and re-layouts: 0 us -> 2.87 us
  other arithmetic: 2.66 us -> 0 us
  Pallas kernels: 81.4 us -> 79.5 us
    broadcast_in_dim x0 -> x1, local copies, waits for them, and re-layouts: none -> 2.87 us  [shards(): return jnp.swapaxes(out, 0, 1)[None]]
    convert_element_type x1 -> x0, other arithmetic: 2.66 us -> none  [shards(): return out.astype(BF).reshape(1, TOK, HEADS, HD)]
    pallas_call x1, Pallas kernels: 81.4 us -> 79.5 us  [shards(): pl.pallas_call(layer_kernel, out_shape=jax.ShapeDtypeStruct((HEADS, TOK,...]
where the time goes in v4:
time: 82.5 us; the launch traced here: 82.4 us
  Pallas kernels  79.5 us (96%)
  local copies, waits for them, and re-layouts  2.87 us (3%)
    pallas_call x1, Pallas kernels, shards(): pl.pallas_call(layer_kernel, out_shape=jax.ShapeDtypeStruct((HEADS, TOK,...  79.5 us
    broadcast_in_dim x1, local copies, waits for them, and re-layouts, shards(): return jnp.swapaxes(out, 0, 1)[None]  2.87 us

profile of v4, /device:TPU:1, one launch (start us, length us, event | category | flops | bytes accessed | tf_op | source)
XLA Modules:
  0.0 82.4 jit_solution(14072257286883710924)
XLA Ops:
  0.0 79.5 %shard_map.73 = bf16[32,128,128]{2,1,0:T(8,128)(2,1)} custom-call(bf16[128,32,128]{2,1,0:T(8,128)(2,1)} %bitcast.17, bf16[128,32,128]{2,1,0:T(8,128)(2,1)} %bitcast.18, bf16[128,32,128]{2,1,0:T(8,128)(2,1)} %bitcast.19, bf16[32,128]{1,0:T(8,128)(2,1)} %bitcast.21, s32[2,128]{1,0:T(2,128)} %bitcast.22, f32[2,128]{1,0:T(2,128)} %bitcast.23, f32[32,128]{1,0:T(8,128)} %bitcast.20), custom_call_target="tpu_custom_call" | custom-call | flops 8000000000 | bytes 6291456 | tf_op jit(solution)/shard_map/pallas_call | solution.py:437
  79.5 2.9 %copy.8 = bf16[1,128,32,128]{3,2,1,0:T(8,128)(2,1)} copy(bf16[1,128,32,128]{3,1,2,0:T(8,128)(2,1)} %bitcast.16) | data formatting | bytes 2097152 | tf_op jit(solution)/shard_map/broadcast_in_dim | solution.py:487

commit v5 on v4

--- a/solution.py
+++ b/solution.py
@@ -14,7 +14,6 @@
 PAIR = 2 * TOK
 TILES = HEADS // 2
 EARLY = 6
-FIRST = 1
 SLAB = TOK + META + HD
 BF = jnp.bfloat16
 F32 = jnp.float32
@@ -162,6 +161,8 @@
     incs,
     locals_,
     parts,
+    decays,
+    reaches,
     kv_s,
     kv_r,
     q_s,
@@ -297,6 +298,19 @@
             [(wide * kept[m : m + 1, :]).astype(BF) for m in range(MEM)], axis=0
         )
         incs[c] = dot(scaled, pair_keys(got, c)).reshape(MEM, HD, HD)
+        middle = 0.5 * total
+        up = jnp.exp(run - middle) * SCALE
+        reach = jnp.exp(run) * SCALE
+        down_h, down_l = split_rows(mask * jnp.exp(middle - run))
+        below = jnp.concatenate([down_h, down_l, down_h, down_l], axis=0).astype(BF)
+        for j, oh in enumerate((oh0, oh1)):
+            up_h, up_l = split_rows(oh * up)
+            above = jnp.concatenate([up_h, up_h, up_l, up_l], axis=0).astype(BF)
+            decay = lax.dot_general(
+                below, above, (((0,), (0,)), ((), ())), preferred_element_type=F32
+            )
+            decays[c, j] = jnp.where(causal, decay, 0.0)
+            reaches[c, j : j + 1, :] = jnp.sum(oh * reach, axis=0, keepdims=True)
 
     def arrived(t):
         others(t, lambda chip, core: kv_copy(chip, core).wait_recv())
@@ -348,24 +362,14 @@
     def inside_tile(c):
         meta = tile_meta(got, c)
         oh0, oh1 = tile_masks(meta)
-        run = sums[pl.ds(c * MEM, MEM), :]
-        middle = 0.5 * run[:, PAIR - 1 : PAIR]
-        up = jnp.exp(run - middle) * SCALE
-        down_h, down_l = split_rows((oh0 + oh1) * jnp.exp(middle - run))
-        below = jnp.concatenate([down_h, down_l, down_h, down_l], axis=0).astype(BF)
         vt = pair_values(got, c)
         qt = jnp.concatenate([q_got[2 * c], q_got[2 * c + 1]], axis=1)
         scores = dot(pair_keys(got, c), qt)
-        reach = jnp.exp(run) * SCALE
+        before = side_by_side(locals_.at[c])
         for j, oh in enumerate((oh0, oh1)):
-            up_h, up_l = split_rows(oh * up)
-            above = jnp.concatenate([up_h, up_h, up_l, up_l], axis=0).astype(BF)
-            decay = lax.dot_general(
-                below, above, (((0,), (0,)), ((), ())), preferred_element_type=F32
-            )
-            weights = jnp.where(causal, scores * decay, 0.0).astype(BF)
-            across = dot(side_by_side(locals_.at[c]), chosen_queries(qt, oh))
-            parts[c, j] = dot(vt, weights) + across * jnp.sum(oh * reach, axis=0, keepdims=True)
+            weights = (scores * decays[c, j]).astype(BF)
+            across = dot(before, chosen_queries(qt, oh))
+            parts[c, j] = dot(vt, weights) + across * reaches[c, j : j + 1, :]
 
     def e_copy(off):
         to, device = at.along(off)
@@ -381,12 +385,14 @@
         loop(1, 8, lambda off: e_copy(off).start())
         e_got[at.z] = e_out[at.z]
 
-    def inside(t):
-        pl.when(t == FIRST)(compose)
-        others(t, lambda chip, core: q_copy(chip, core).wait_recv())
-        inside_tile(at.source(t, 0)[0])
-
-    loop(0, TILES, inside)
+    def inside(i):
+        for t in (2 * i, 2 * i + 1):
+            others(t, lambda chip, core: q_copy(chip, core).wait_recv())
+        for t in (2 * i, 2 * i + 1):
+            inside_tile(at.source(t, 0)[0])
+
+    compose()
+    loop(0, TILES // 2, inside)
     for copy in (kv_copy, q_copy):
         sent = lambda chip, core, copy=copy: copy(chip, core).wait_send()
         loop(0, TILES, lambda t, sent=sent: others(t, sent))
@@ -466,6 +472,8 @@
             pltpu.VMEM((TILES, MEM, HD, HD), F32),
             pltpu.VMEM((TILES, MEM, HD, HD), BF),
             pltpu.VMEM((TILES, 2, HD, PAIR), F32),
+            pltpu.VMEM((TILES, 2, PAIR, PAIR), F32),
+            pltpu.VMEM((TILES, 8, PAIR), F32),
             *sems,
             pltpu.SemaphoreType.DMA((7,)),
         ],

time: 82.5 us -> 78.9 us (0.956)
  Pallas kernels: 79.5 us -> 75.9 us
    pallas_call x1, Pallas kernels: 79.5 us -> 75.9 us  [shards(): pl.pallas_call(layer_kernel, out_shape=jax.ShapeDtypeStruct((HEADS, TOK,...]
where the time goes in v5:
time: 78.9 us; the launch traced here: 78.8 us
  Pallas kernels  75.9 us (96%)
  local copies, waits for them, and re-layouts  2.87 us (4%)
    pallas_call x1, Pallas kernels, shards(): pl.pallas_call(layer_kernel, out_shape=jax.ShapeDtypeStruct((HEADS, TOK,...  75.9 us
    broadcast_in_dim x1, local copies, waits for them, and re-layouts, shards(): return jnp.swapaxes(out, 0, 1)[None]  2.87 us

profile of v5, /device:TPU:1, one launch (start us, length us, event | category | flops | bytes accessed | tf_op | source)
XLA Modules:
  0.0 78.8 jit_solution(15463432643981997535)
XLA Ops:
  0.0 75.9 %shard_map.73 = bf16[32,128,128]{2,1,0:T(8,128)(2,1)} custom-call(bf16[128,32,128]{2,1,0:T(8,128)(2,1)} %bitcast.17, bf16[128,32,128]{2,1,0:T(8,128)(2,1)} %bitcast.18, bf16[128,32,128]{2,1,0:T(8,128)(2,1)} %bitcast.19, bf16[32,128]{1,0:T(8,128)(2,1)} %bitcast.21, s32[2,128]{1,0:T(2,128)} %bitcast.22, f32[2,128]{1,0:T(2,128)} %bitcast.23, f32[32,128]{1,0:T(8,128)} %bitcast.20), custom_call_target="tpu_custom_call" | custom-call | flops 8000000000 | bytes 6291456 | tf_op jit(solution)/shard_map/pallas_call | solution.py:443
  75.9 2.9 %copy.8 = bf16[1,128,32,128]{3,2,1,0:T(8,128)(2,1)} copy(bf16[1,128,32,128]{3,1,2,0:T(8,128)(2,1)} %bitcast.16) | data formatting | bytes 2097152 | tf_op jit(solution)/shard_map/broadcast_in_dim | solution.py:495

commit v6 on v5

--- a/solution.py
+++ b/solution.py
@@ -318,21 +318,24 @@
 
     loop(0, TILES, arrived)
 
-    def add_total(c, base):
-        at_c = pl.ds(c * MEM, MEM)
-        total = totals[at_c, :]
-        bases[at_c, :] = base
-        totals[at_c, :] = jnp.exp(total)
-        return base + total
-
-    whole = lax.fori_loop(0, TILES, add_total, jnp.zeros((MEM, HD), F32))
+    whole = jnp.zeros((MEM, HD), F32)
+    for c in range(TILES):
+        lines = slice(c * MEM, (c + 1) * MEM)
+        bases[lines, :] = whole
+        total = totals[lines, :]
+        totals[lines, :] = jnp.exp(total)
+        whole = whole + total
     left_h, left_l = split_rows(jnp.exp(whole))
     left[0:MEM, :] = left_h
     left[MEM:, :] = left_l
 
-    def z_copy(off):
+    halves = (pl.ds(0, META + HD // 2), pl.ds(META + HD // 2, HD // 2))
+    e_halves = (pl.ds(0, HD // 2), pl.ds(HD // 2, HD // 2))
+
+    def z_copy(off, half):
         to, device = at.along(off)
-        return remote(z_out.at[to], z_got.at[at.z], z_sem, off, device)
+        rows = halves[half]
+        return remote(z_out.at[to, rows], z_got.at[at.z, rows], z_sem, 2 * off + half, device)
 
     def memory_states(m):
         def four(i, run):
@@ -343,18 +346,19 @@
             return run
 
         run = lax.fori_loop(0, TILES // 4, four, jnp.zeros((HD, HD), F32))
-        z_out[m, 0:HD, :] = run.astype(BF)
+        z_out[m, META:, :] = run.astype(BF)
         lines = left[pl.ds(m, 1), :], left[pl.ds(MEM + m, 1), :]
-        z_out[m, HD:, :] = jnp.where(row == 0, *lines).astype(BF)
+        z_out[m, 0:META, :] = jnp.where(row == 0, *lines).astype(BF)
 
     def send_states(off):
         memory_states(at.along(off)[0])
-        z_copy(off).start()
+        z_copy(off, 0).start()
         start_pair(q_copy, 2 * off - 1)
         start_pair(q_copy, 2 * off)
 
     q_copy(0, 1).start()
     loop(1, 8, send_states)
+    loop(1, 8, lambda off: z_copy(off, 1).start())
     start_pair(q_copy, TILES - 1)
     memory_states(at.z)
     z_got[at.z] = z_out[at.z]
@@ -371,19 +375,22 @@
             across = dot(before, chosen_queries(qt, oh))
             parts[c, j] = dot(vt, weights) + across * reaches[c, j : j + 1, :]
 
-    def e_copy(off):
+    def e_copy(off, half):
         to, device = at.along(off)
-        return remote(e_out.at[to], e_got.at[at.z], e_sem, off, device)
-
-    def compose():
-        loop(1, 8, lambda off: z_copy(off).wait_recv())
-        entering = jnp.zeros((HD, HD), F32)
+        rows = e_halves[half]
+        return remote(e_out.at[to, rows], e_got.at[at.z, rows], e_sem, 2 * off + half, device)
+
+    def compose(half):
+        loop(1, 8, lambda off: z_copy(off, half).wait_recv())
+        entering = jnp.zeros((HD // 2, HD), F32)
+        low = half * (HD // 2)
+        rows = slice(low, low + HD // 2)
+        given = slice(META + low, META + low + HD // 2)
         for z in range(8):
-            e_out[z] = entering.astype(BF)
-            kept = z_got[z, HD : HD + META, :].astype(F32)
-            entering = entering * (kept[0:1, :] + kept[1:2, :]) + z_got[z, 0:HD, :].astype(F32)
-        loop(1, 8, lambda off: e_copy(off).start())
-        e_got[at.z] = e_out[at.z]
+            e_out[z, rows, :] = entering.astype(BF)
+            kept = z_got[z, 0:META, :].astype(F32)
+            entering = entering * (kept[0:1, :] + kept[1:2, :]) + z_got[z, given, :].astype(F32)
+        loop(1, 8, lambda off: e_copy(off, half).start())
 
     def inside(i):
         for t in (2 * i, 2 * i + 1):
@@ -391,14 +398,16 @@
         for t in (2 * i, 2 * i + 1):
             inside_tile(at.source(t, 0)[0])
 
-    compose()
+    compose(0)
+    compose(1)
+    e_got[at.z] = e_out[at.z]
     loop(0, TILES // 2, inside)
     for copy in (kv_copy, q_copy):
         sent = lambda chip, core, copy=copy: copy(chip, core).wait_send()
         loop(0, TILES, lambda t, sent=sent: others(t, sent))
-    loop(1, 8, lambda off: z_copy(off).wait_send())
-
-    loop(1, 8, lambda off: e_copy(off).wait_recv())
+    loop(1, 8, lambda off: [z_copy(off, half).wait_send() for half in (0, 1)])
+
+    loop(1, 8, lambda off: [e_copy(off, half).wait_recv() for half in (0, 1)])
     gain = gain_here[pl.ds(me, 1), :]
 
     def finish_tile(c):
@@ -430,7 +439,7 @@
     loop(0, TILES, finish)
     own = pltpu.make_async_copy(o_out.at[me], out_ref.at[me], in_s.at[0])
     own.start()
-    loop(1, 8, lambda off: e_copy(off).wait_send())
+    loop(1, 8, lambda off: [e_copy(off, half).wait_send() for half in (0, 1)])
     own.wait()
     every = pl.ds(0, HEADS - 1)
     whole_out = remote(o_out.at[every], out_ref.at[every], o_sem, 0, at.target(0, 1)[2])
@@ -439,7 +448,7 @@
 
 
 def shards(queries, keys, values, log_decay, routes, route_weight, gain):
-    sems = [pltpu.SemaphoreType.DMA((HEADS,))] * 4 + [pltpu.SemaphoreType.DMA((1,))] * 2 + [pltpu.SemaphoreType.DMA((8,))] * 4
+    sems = [pltpu.SemaphoreType.DMA((HEADS,))] * 4 + [pltpu.SemaphoreType.DMA((1,))] * 2 + [pltpu.SemaphoreType.DMA((16,))] * 4
     out = pl.pallas_call(
         layer_kernel,
         out_shape=jax.ShapeDtypeStruct((HEADS, TOK, HD), BF),

time: 78.9 us -> 79.3 us (level)
  no operation moved by 1% of the time
where the time goes in v6:
time: 79.3 us; the launch traced here: 79.2 us
  Pallas kernels  76.3 us (96%)
  local copies, waits for them, and re-layouts  2.87 us (4%)
    pallas_call x1, Pallas kernels, shards(): pl.pallas_call(layer_kernel, out_shape=jax.ShapeDtypeStruct((HEADS, TOK,...  76.3 us
    broadcast_in_dim x1, local copies, waits for them, and re-layouts, shards(): return jnp.swapaxes(out, 0, 1)[None]  2.87 us

profile of v6, /device:TPU:1, one launch (start us, length us, event | category | flops | bytes accessed | tf_op | source)
XLA Modules:
  0.0 79.2 jit_solution(6080121143629408265)
XLA Ops:
  0.0 76.3 %shard_map.73 = bf16[32,128,128]{2,1,0:T(8,128)(2,1)} custom-call(bf16[128,32,128]{2,1,0:T(8,128)(2,1)} %bitcast.17, bf16[128,32,128]{2,1,0:T(8,128)(2,1)} %bitcast.18, bf16[128,32,128]{2,1,0:T(8,128)(2,1)} %bitcast.19, bf16[32,128]{1,0:T(8,128)(2,1)} %bitcast.21, s32[2,128]{1,0:T(2,128)} %bitcast.22, f32[2,128]{1,0:T(2,128)} %bitcast.23, f32[32,128]{1,0:T(8,128)} %bitcast.20), custom_call_target="tpu_custom_call" | custom-call | flops 8000000000 | bytes 6291456 | tf_op jit(solution)/shard_map/pallas_call | solution.py:452
  76.3 2.9 %copy.8 = bf16[1,128,32,128]{3,2,1,0:T(8,128)(2,1)} copy(bf16[1,128,32,128]{3,1,2,0:T(8,128)(2,1)} %bitcast.16) | data formatting | bytes 2097152 | tf_op jit(solution)/shard_map/broadcast_in_dim | solution.py:504

commit v7 on v6

--- a/solution.py
+++ b/solution.py
@@ -14,6 +14,7 @@
 PAIR = 2 * TOK
 TILES = HEADS // 2
 EARLY = 6
+ENOUGH = 12
 SLAB = TOK + META + HD
 BF = jnp.bfloat16
 F32 = jnp.float32
@@ -314,6 +315,11 @@
 
     def arrived(t):
         others(t, lambda chip, core: kv_copy(chip, core).wait_recv())
+
+        @pl.when(t == ENOUGH)
+        def _():
+            loop(0, TILES, lambda chip: start_pair(q_copy, chip))
+
         gather_tile(at.source(t, 0)[0])
 
     loop(0, TILES, arrived)
@@ -353,13 +359,9 @@
     def send_states(off):
         memory_states(at.along(off)[0])
         z_copy(off, 0).start()
-        start_pair(q_copy, 2 * off - 1)
-        start_pair(q_copy, 2 * off)
-
-    q_copy(0, 1).start()
+
     loop(1, 8, send_states)
     loop(1, 8, lambda off: z_copy(off, 1).start())
-    start_pair(q_copy, TILES - 1)
     memory_states(at.z)
     z_got[at.z] = z_out[at.z]
 

time: 79.3 us -> 78.6 us (level)
  no operation moved by 1% of the time
where the time goes in v7:
time: 78.6 us; the launch traced here: 78.4 us
  Pallas kernels  75.6 us (96%)
  local copies, waits for them, and re-layouts  2.87 us (4%)
    pallas_call x1, Pallas kernels, shards(): pl.pallas_call(layer_kernel, out_shape=jax.ShapeDtypeStruct((HEADS, TOK,...  75.6 us
    broadcast_in_dim x1, local copies, waits for them, and re-layouts, shards(): return jnp.swapaxes(out, 0, 1)[None]  2.87 us

profile of v7, /device:TPU:1, one launch (start us, length us, event | category | flops | bytes accessed | tf_op | source)
XLA Modules:
  0.0 78.4 jit_solution(1745983936791667359)
XLA Ops:
  0.0 75.6 %shard_map.73 = bf16[32,128,128]{2,1,0:T(8,128)(2,1)} custom-call(bf16[128,32,128]{2,1,0:T(8,128)(2,1)} %bitcast.17, bf16[128,32,128]{2,1,0:T(8,128)(2,1)} %bitcast.18, bf16[128,32,128]{2,1,0:T(8,128)(2,1)} %bitcast.19, bf16[32,128]{1,0:T(8,128)(2,1)} %bitcast.21, s32[2,128]{1,0:T(2,128)} %bitcast.22, f32[2,128]{1,0:T(2,128)} %bitcast.23, f32[32,128]{1,0:T(8,128)} %bitcast.20), custom_call_target="tpu_custom_call" | custom-call | flops 8000000000 | bytes 6291456 | tf_op jit(solution)/shard_map/pallas_call | solution.py:454
  75.6 2.9 %copy.8 = bf16[1,128,32,128]{3,2,1,0:T(8,128)(2,1)} copy(bf16[1,128,32,128]{3,1,2,0:T(8,128)(2,1)} %bitcast.16) | data formatting | bytes 2097152 | tf_op jit(solution)/shard_map/broadcast_in_dim | solution.py:506

commit v8 on v7

--- a/solution.py
+++ b/solution.py
@@ -14,6 +14,7 @@
 PAIR = 2 * TOK
 TILES = HEADS // 2
 EARLY = 6
+AHEAD = 2
 ENOUGH = 12
 SLAB = TOK + META + HD
 BF = jnp.bfloat16
@@ -394,15 +395,18 @@
             entering = entering * (kept[0:1, :] + kept[1:2, :]) + z_got[z, given, :].astype(F32)
         loop(1, 8, lambda off: e_copy(off, half).start())
 
+    def compose_both():
+        compose(0)
+        compose(1)
+        e_got[at.z] = e_out[at.z]
+
     def inside(i):
+        pl.when(i == AHEAD)(compose_both)
         for t in (2 * i, 2 * i + 1):
             others(t, lambda chip, core: q_copy(chip, core).wait_recv())
         for t in (2 * i, 2 * i + 1):
             inside_tile(at.source(t, 0)[0])
 
-    compose(0)
-    compose(1)
-    e_got[at.z] = e_out[at.z]
     loop(0, TILES // 2, inside)
     for copy in (kv_copy, q_copy):
         sent = lambda chip, core, copy=copy: copy(chip, core).wait_send()

time: 78.6 us -> 78 us (level)
  no operation moved by 1% of the time
where the time goes in v8:
time: 78 us; the launch traced here: 77.9 us
  Pallas kernels  75 us (96%)
  local copies, waits for them, and re-layouts  2.87 us (4%)
    pallas_call x1, Pallas kernels, shards(): pl.pallas_call(layer_kernel, out_shape=jax.ShapeDtypeStruct((HEADS, TOK,...  75 us
    broadcast_in_dim x1, local copies, waits for them, and re-layouts, shards(): return jnp.swapaxes(out, 0, 1)[None]  2.87 us

profile of v8, /device:TPU:1, one launch (start us, length us, event | category | flops | bytes accessed | tf_op | source)
XLA Modules:
  0.0 77.9 jit_solution(16600150470128880292)
XLA Ops:
  0.0 75.0 %shard_map.73 = bf16[32,128,128]{2,1,0:T(8,128)(2,1)} custom-call(bf16[128,32,128]{2,1,0:T(8,128)(2,1)} %bitcast.17, bf16[128,32,128]{2,1,0:T(8,128)(2,1)} %bitcast.18, bf16[128,32,128]{2,1,0:T(8,128)(2,1)} %bitcast.19, bf16[32,128]{1,0:T(8,128)(2,1)} %bitcast.21, s32[2,128]{1,0:T(2,128)} %bitcast.22, f32[2,128]{1,0:T(2,128)} %bitcast.23, f32[32,128]{1,0:T(8,128)} %bitcast.20), custom_call_target="tpu_custom_call" | custom-call | flops 8000000000 | bytes 6291456 | tf_op jit(solution)/shard_map/pallas_call | solution.py:458
  75.0 2.9 %copy.8 = bf16[1,128,32,128]{3,2,1,0:T(8,128)(2,1)} copy(bf16[1,128,32,128]{3,1,2,0:T(8,128)(2,1)} %bitcast.16) | data formatting | bytes 2097152 | tf_op jit(solution)/shard_map/broadcast_in_dim | solution.py:510
